TPU v7x, 128 devices: a whole 4x4x4 slice. The times are simulated.
128 devices in a mesh: aux: 4 (over x), pair: 32 (over z, y, core).
Axes of the slice: x: 4, y: 4, z: 4, core: 2. Of those that a mesh axis runs over, the one named last changes fastest.
Arguments:
- three_index: bfloat16 [512, 256, 2048], P('pair', None, 'aux'), may hold values from -0.875 to 0.875
- fock_diag: float32 [512], replicated, may hold values from -1.2 to -0.3
- pair_occ: int32 [992, 2], P('pair'), may hold values from 0 to 511, as said below
- pno_count: int32 [992], P('pair'), may hold values from 32 to 128
- pno_energy: float32 [992, 128], P('pair'), may hold values from 0.3 to 3
- pno_coef: bfloat16 [992, 2, 256, 128], P('pair'), may hold values from -0.375 to 0.375
Outputs:
- pair_energy: float32 [992], P('pair')
- grad_ints: float32 [512, 256, 2048], P('pair', None, 'aux')
Inputs may be any that keep to these rules, and one draw needn't show every extreme that they name: `pair_occ`: orbital o belongs to the block o // 16. Among the 62 orbitals named by the pairs of one aligned block of 31 rows, at most 2 belong to any one orbital block, and one orbital block receives exactly 2 from every such row block; i may equal j.
All inputs are finite; a program needn't handle non-finite values.
Results may differ from a plain program's by a relative error of at most 0.0061.
Values may be sent and summed in bfloat16 or wider, within the bound.
A program may use at most 128 MiB of HBM per device.

v0:
```python
import jax
import jax.numpy as jnp
from jax import lax
from jax.sharding import PartitionSpec as P


def local(three_index, fock_diag, pair_occ, pno_count, pno_energy, pno_coef):
    groups = lax.axis_size("pair")
    occ_dev = three_index.shape[0]
    width_dom = three_index.shape[1]
    width_aux = three_index.shape[2]
    pair_dev = pair_occ.shape[0]
    width_pno = pno_coef.shape[3]
    halves = 2 * pair_dev
    capacity = max(2, halves // groups + 1)
    slots = groups * capacity
    occ_flat = pair_occ.reshape(halves)
    owner_of = occ_flat // occ_dev
    local_index = occ_flat % occ_dev
    owner_hot = (owner_of[:, None] == jnp.arange(groups, dtype=jnp.int32)[None, :]).astype(
        jnp.int32
    )
    before = jnp.cumsum(owner_hot, axis=0) - owner_hot
    rank_in = jnp.sum(before * owner_hot, axis=1)
    slot_of = owner_of * capacity + rank_in
    request = jnp.zeros((slots,), jnp.int32).at[slot_of].set(local_index + 1)
    arrived = lax.all_to_all(
        request.reshape(groups, capacity), "pair", split_axis=0, concat_axis=0, tiled=True
    ).reshape(slots)
    is_live = arrived > 0
    row_index = jnp.maximum(arrived - 1, 0)
    selected = jnp.take(three_index, row_index, axis=0)
    selected = jnp.where(is_live[:, None, None], selected, jnp.zeros_like(selected))
    coef_half = pno_coef.reshape(halves, width_dom, width_pno)
    rows_back = lax.all_to_all(
        selected.reshape(groups, capacity, width_dom, width_aux),
        "pair",
        split_axis=0,
        concat_axis=0,
        tiled=True,
    )
    mine = jnp.take(rows_back.reshape(slots, width_dom, width_aux), slot_of, axis=0)
    projected = jnp.einsum(
        "hdp,hdq->hpq", coef_half, mine, preferred_element_type=jnp.float32
    ).astype(jnp.bfloat16)
    paired = projected.reshape(pair_dev, 2, width_pno, width_aux)
    rows_i = paired[:, 0]
    rows_j = paired[:, 1]
    partial_sum = jnp.einsum("kpq,krq->kpr", rows_i, rows_j, preferred_element_type=jnp.float32)
    coupling = lax.psum(partial_sum, "aux")
    fock_i = jnp.take(fock_diag, pair_occ[:, 0])
    fock_j = jnp.take(fock_diag, pair_occ[:, 1])
    denom = pno_energy[:, :, None] + pno_energy[:, None, :] - (fock_i + fock_j)[:, None, None]
    in_pno = jnp.arange(width_pno, dtype=jnp.int32)[None, :] < pno_count[:, None]
    both_in = in_pno[:, :, None] & in_pno[:, None, :]
    amplitude = jnp.where(both_in, -coupling / denom, jnp.float32(0.0))
    mixed = 2.0 * amplitude - jnp.swapaxes(amplitude, 1, 2)
    energy = jnp.sum(coupling * mixed, axis=(1, 2)) / (width_pno * width_pno)
    weights = mixed.astype(jnp.bfloat16)
    gamma_i = jnp.einsum(
        "kab,kbq->kaq", weights, rows_j, preferred_element_type=jnp.float32
    ).astype(jnp.bfloat16)
    gamma_j = jnp.einsum(
        "kba,kbq->kaq", weights, rows_i, preferred_element_type=jnp.float32
    ).astype(jnp.bfloat16)
    gamma = jnp.stack([gamma_i, gamma_j], axis=1).reshape(halves, width_pno, width_aux)
    dom_terms = jnp.einsum(
        "hdp,hpq->hdq", coef_half, gamma, preferred_element_type=jnp.float32
    ).astype(jnp.bfloat16)
    term_send = jnp.zeros((slots, width_dom, width_aux), jnp.bfloat16).at[slot_of].set(dom_terms)
    terms = lax.all_to_all(
        term_send.reshape(groups, capacity, width_dom, width_aux),
        "pair",
        split_axis=0,
        concat_axis=0,
        tiled=True,
    )
    terms = terms.reshape(slots, width_dom, width_aux)
    occ_hot = (row_index[None, :] == jnp.arange(occ_dev, dtype=jnp.int32)[:, None]) & is_live[
        None, :
    ]
    grad = jnp.dot(
        occ_hot.astype(jnp.bfloat16),
        terms.reshape(slots, width_dom * width_aux),
        preferred_element_type=jnp.float32,
    )
    return (energy, grad.reshape(occ_dev, width_dom, width_aux))


def solution(mesh):
    placed = (
        P("pair", None, "aux"),
        P(),
        P("pair", None),
        P("pair"),
        P("pair", None),
        P("pair", None, None, None),
    )
    return jax.shard_map(
        local,
        mesh=mesh,
        in_specs=placed,
        out_specs=(P("pair"), P("pair", None, "aux")),
        check_vma=False,
    )
```

profile of v0, /device:TPU:0, one launch (start us, length us, event | category | flops | bytes accessed | tf_op | source)
XLA Modules:
  0.0 716.0 jit_solution(3268946440946229828)
XLA Ops:
  7.2 0.0 copy-start
  7.2 0.8 copy.56
  8.0 0.1 reshape.245
  8.1 0.1 reshape.244
  8.2 0.1 fusion.14
  8.3 0.1 reduce_window_sum.11
  8.4 0.2 select_reduce_fusion
  8.6 0.8 scatter_custom_fusion
  9.3 0.1 all_to_all.12
  9.4 15.6 %all_to_all.19 = s32[32,1,2]{2,1,0:T(1,128)S(1)} all-to-all(s32[32,1,2]{2,1,0:T(1,128)S(1)} %bitcast.90), channel_id=1, replica_groups=mesh['aux'=4,'pair'=32] {'pair'}, dimensions={0} | all-to-all | bytes 512 | tf_op jit(solution)/shard_map/all_to_all | solution.py:27
  25.0 0.1 copy.59
  25.1 0.1 copy.62
  25.2 0.1 copy.60
  25.3 0.1 copy.63
  25.4 0.1 reshape.269
  25.5 9.8 %gather_fusion = bf16[64,256,512]{2,1,0:T(8,128)(2,1)} fusion(bf16[16,256,512]{2,1,0:T(8,128)(2,1)} %param.8, s32[1024]{0:T(1024)S(1)} %pad_clamp_fusion.3), kind=kCustom, calls=%fused_computation.2 | custom fusion | bytes 33554688 | tf_op jit(solution)/shard_map/jit(_take)/gather | solution.py:32
  35.3 14.3 %select_select_fusion = bf16[32,2,256,512]{3,2,1,0:T(8,128)(2,1)} fusion(bf16[32,2,256,512]{3,2,1,0:T(8,128)(2,1)} %bitcast.81, pred[32,2]{1,0:T(8,128)(4,1)S(1)} %copy.62, pred[32,2]{1,0:T(8,128)(4,1)S(1)} %copy.60), kind=kLoop, calls=%fused_computation.9 | loop fusion | flops 16777216 | bytes 33554560 | tf_op jit(solution)/shard_map/jit(_where)/select_n | solution.py:33
  49.6 5.2 all-to-all-start.1
  54.8 0.2 all-reduce.2.cloned.1.call-start
  55.1 213.0 %all-to-all-done.1 = bf16[32,2,256,512]{3,2,1,0:T(8,128)(2,1)} async-done(((bf16[32,2,256,512]{3,2,1,0:T(8,128)(2,1)}), bf16[32,2,256,512]{3,2,1,0:T(8,128)(2,1)}, u32[]{:S(2)}, u32[]{:S(2)}) %all-to-all-start.1) | async-done | bytes 16777248 | tf_op jit(solution)/shard_map/all_to_all | solution.py:35
  268.0 13.3 %gather_fusion.1 = bf16[62,256,512]{2,1,0:T(8,128)(2,1)} fusion(bf16[64,256,512]{2,1,0:T(8,128)(2,1)} %bitcast.6, s32[1024]{0:T(1024)S(1)} %pad_clamp_fusion.2), kind=kCustom, calls=%fused_computation.3 | custom fusion | bytes 32506104 | tf_op jit(solution)/shard_map/jit(_take)/gather | solution.py:42
  281.3 11.8 %fusion.7 = bf16[62,512,128]{2,1,0:T(8,128)(2,1)} fusion(bf16[62,256,128]{2,1,0:T(8,128)(2,1)} %bitcast.83, bf16[62,256,512]{2,1,0:T(8,128)(2,1)} %gather_fusion.1, pred[62]{0:T(512)(128)(4,1)S(1)} %compare_and_fusion), kind=kOutput, calls=%fused_computation.16 | convolution fusion | flops 2092564480 | bytes 28442686 | tf_op jit(solution)/shard_map/hdp,hdq->hpq/dot_general | solution.py:43
  293.1 0.0 copy-start.3
  293.1 0.0 copy-start.4
  293.1 0.0 copy-start.2
  293.1 6.0 fusion.11
  299.1 0.0 all-reduce.2.cloned.1.call-update
  299.1 0.0 copy-done.3
  299.2 0.0 copy-done
  299.2 0.7 gather_fusion.3
  299.9 0.7 gather_fusion.2
  300.6 0.0 copy-done.4
  300.6 0.1 iota_compare_fusion.1
  300.7 52.8 %all-reduce.2.cloned.1.call-done = f32[31,128,128]{2,1,0:T(8,128)} async-done(((f32[31,128,128]{2,1,0:T(8,128)}), f32[31,128,128]{2,1,0:T(8,128)}) %all-reduce.2.cloned.1.call-update) | async-done | bytes 2031632 | tf_op jit(solution)/shard_map/psum | solution.py:50
  353.5 2.3 copy.67
  355.8 0.0 copy-done.2
  355.8 2.7 broadcast_multiply_fusion
  358.5 2.9 copy.68
  361.4 0.0 slice-start
  361.4 4.0 fusion.13
  365.4 0.0 slice-start.1
  365.4 5.5 convert_bitcast_fusion.1
  370.8 0.0 slice-done
  370.8 0.0 slice-done.1
  370.8 3.2 convert_bitcast_fusion.2
  374.0 4.1 pad_maximum_fusion
  378.2 4.3 copy.71
  382.4 11.3 %convert_bitcast_fusion = bf16[62,256,512]{1,2,0:T(8,128)(2,1)} fusion(bf16[62,128,512]{2,1,0:T(8,128)(2,1)} %bitcast.82, bf16[62,256,128]{2,1,0:T(8,128)(2,1)} %bitcast.84), kind=kOutput, calls=%fused_computation.10 | convolution fusion | flops 2088501248 | bytes 28442624 | tf_op jit(solution)/shard_map/hdp,hpq->hdq/dot_general | solution.py:67
  393.7 21.9 %copy.73 = bf16[62,256,512]{2,1,0:T(8,128)(2,1)} copy(bf16[62,256,512]{1,2,0:T(8,128)(2,1)} %convert_bitcast_fusion) | data formatting | bytes 32505856 | tf_op jit(solution)/shard_map/convert_element_type | solution.py:69
  415.6 5.9 broadcast.266
  421.5 41.8 %scatter_fusion = bf16[64,256,512]{2,1,0:T(8,128)(2,1)} fusion(bf16[64,256,512]{2,1,0:T(8,128)(2,1)} %broadcast.266, s32[62]{0:T(128)S(1)} %fusion.22, bf16[62,256,512]{2,1,0:T(8,128)(2,1)} %copy.73), kind=kCustom, calls=%fused_computation.5 | custom fusion | bytes 48759032 | tf_op jit(solution)/shard_map/scatter | solution.py:70
  463.3 7.6 %all-to-all-start.2 = ((bf16[32,2,256,512]{3,2,1,0:T(8,128)(2,1)}), bf16[32,2,256,512]{3,2,1,0:T(8,128)(2,1)}, u32[]{:S(2)}, u32[]{:S(2)}) async-start(bf16[32,2,256,512]{3,2,1,0:T(8,128)(2,1)} %bitcast.80), calls=%async_computation.2 | async-start | bytes 33554432 | tf_op jit(solution)/shard_map/all_to_all | solution.py:71
  470.9 0.1 copy.69
  471.0 0.1 gt.19
  471.1 0.5 broadcast_multiply_fusion.1
  471.6 212.5 %all-to-all-done.2 = bf16[32,2,256,512]{3,2,1,0:T(8,128)(2,1)} async-done(((bf16[32,2,256,512]{3,2,1,0:T(8,128)(2,1)}), bf16[32,2,256,512]{3,2,1,0:T(8,128)(2,1)}, u32[]{:S(2)}, u32[]{:S(2)}) %all-to-all-start.2) | async-done | bytes 16777248 | tf_op jit(solution)/shard_map/all_to_all | solution.py:71
  684.1 0.0 copy-start.1
  684.1 16.8 %fusion = f32[16,256,512]{2,0,1:T(8,128)S(1)} fusion(s32[64]{0:T(128)S(1)} %reshape.269, pred[64]{0:T(512)(128)(4,1)S(1)} %gt.19, bf16[8,8,256,512]{3,2,1,0:T(8,128)(2,1)} %bitcast.32), kind=kOutput, calls=%fused_computation.6 | convolution fusion | flops 268437504 | bytes 25166144 | tf_op jit(solution)/shard_map/dot_general | solution.py:82
  700.9 8.3 %copy.75 = f32[16,256,512]{2,1,0:T(8,128)} copy(f32[16,256,512]{2,0,1:T(8,128)S(1)} %fusion) | data formatting | bytes 16777216
  709.1 0.0 copy-done.1
  (11 shorter events, 0.1 us)
Async XLA Ops:
  7.2 292.0 %copy-start = (f32[512]{0:T(512)S(1)}, f32[512]{0:T(512)}, u32[]{:S(2)}) copy-start(f32[512]{0:T(512)} %param.9) | copy-start | bytes 6148
  49.6 218.4 %all-to-all-start.1 = ((bf16[32,2,256,512]{3,2,1,0:T(8,128)(2,1)}), bf16[32,2,256,512]{3,2,1,0:T(8,128)(2,1)}, u32[]{:S(2)}, u32[]{:S(2)}) async-start(bf16[32,2,256,512]{3,2,1,0:T(8,128)(2,1)} %select_select_fusion), calls=%async_computation.1 | async-start | bytes 33554432 | tf_op jit(solution)/shard_map/all_to_all | solution.py:35
  54.8 298.7 %all-reduce.2.cloned.1.call-start = ((), (), s32[]{:S(2)}) async-start(), calls=%async_computation.3 | async-start | bytes 4063232 | tf_op jit(solution)/shard_map/psum | solution.py:50
  293.1 6.0 copy-start.3
  293.1 7.5 %copy-start.4 = (s32[31]{0:T(128)S(1)}, s32[31]{0:T(128)}, u32[]{:S(2)}) copy-start(s32[31]{0:T(128)} %param.11) | copy-start | bytes 376
  293.1 62.7 %copy-start.2 = (f32[31,128]{1,0:T(8,128)S(1)}, f32[31,128]{1,0:T(8,128)}, u32[]{:S(2)}) copy-start(f32[31,128]{1,0:T(8,128)} %param.12) | copy-start | bytes 47620
  361.4 9.5 %slice-start = ((s8[8126464]{0:T(1024)(128)(4,1)}), s8[4194304]{0:T(1024)(128)(4,1)S(1)}, s32[]{:S(2)}) async-start(s8[8126464]{0:T(1024)(128)(4,1)} %bitcast.87), calls=%async_computation.4 | async-start | bytes 8388608
  365.4 5.5 slice-start.1
  463.3 220.8 %all-to-all-start.2 = ((bf16[32,2,256,512]{3,2,1,0:T(8,128)(2,1)}), bf16[32,2,256,512]{3,2,1,0:T(8,128)(2,1)}, u32[]{:S(2)}, u32[]{:S(2)}) async-start(bf16[32,2,256,512]{3,2,1,0:T(8,128)(2,1)} %bitcast.80), calls=%async_computation.2 | async-start | bytes 33554432 | tf_op jit(solution)/shard_map/all_to_all | solution.py:71
  684.1 25.0 %copy-start.1 = (f32[512]{0:T(512)S(1)}, f32[512]{0:T(512)}, u32[]{:S(2)}) copy-start(f32[512]{0:T(512)} %param.9) | copy-start | bytes 6148
Sparse Core Ops, SparseCore 0:
  299.3 54.1 all-reduce.1
where the time goes:
time: 717 us; the launch traced here: 716 us
  waiting for transfers between devices  478 us (67%)
  local copies, waits for them, and re-layouts  114 us (16%)
  matrix products  54.5 us (8%)
  other arithmetic  26.1 us (4%)
  blocking collectives  15.6 us (2%)
  between operations  14.2 us (2%)
  starting transfers between devices  13 us (2%)
    all_to_all x1, waiting for transfers between devices, local(): lax.all_to_all(selected.reshape(groups, capacity, width_dom, width_aux),...  213 us
    all_to_all x1, waiting for transfers between devices, local(): lax.all_to_all(term_send.reshape(groups, capacity, width_dom, width_aux),...  212 us
    psum x1, waiting for transfers between devices, local(): coupling = lax.psum(partial_sum, 'aux')  52.8 us
    scatter x1, local copies, waits for them, and re-layouts, local(): jnp.zeros((slots, width_dom, width_aux), jnp.bfloat16).at[slot_of]  41.8 us
    convert_element_type x1, local copies, waits for them, and re-layouts, local(): dom_terms = jnp.einsum('hdp,hpq->hdq', coef_half, gamma, preferred_elemen...  21.9 us
    dot_general x1, matrix products, local(): jnp.dot(occ_hot.astype(jnp.bfloat16), terms.reshape(slots, width_dom * wi...  16.8 us
    all_to_all x1, blocking collectives, local(): lax.all_to_all(request.reshape(groups, capacity), 'pair', split_axis=0, c...  15.6 us
  transfers between devices with their start and end apart: 3, of which 3 were waited for; matrix products, arithmetic and copies ran while one was open for 0% of the time, Pallas kernels for 0%

commit v1 on v0

v1 whole, which is shorter than its diff:
```python
import functools

import jax
import jax.numpy as jnp
from jax import lax
from jax.experimental import pallas as pl
from jax.experimental.pallas import tpu as pltpu
from jax.sharding import PartitionSpec as P

CAPACITY = 2
STEP_SLOTS = 4
VMEM_LIMIT = 48 << 20


def plan_slots(pair_occ, groups, occ_dev):
    occ_flat = pair_occ.reshape(-1)
    halves = occ_flat.shape[0]
    owner = occ_flat // occ_dev
    half_ids = jnp.arange(halves, dtype=jnp.int32)
    earlier = (owner[None, :] == owner[:, None]) & (half_ids[None, :] < half_ids[:, None])
    rank = jnp.sum(earlier.astype(jnp.int32), axis=1)
    slot_of = owner * CAPACITY + rank
    hot = (slot_of[None, :] == jnp.arange(groups * CAPACITY, dtype=jnp.int32)[:, None]).astype(jnp.int32)
    half_of = jnp.sum(hot * (half_ids + 1)[None, :], axis=1) - 1
    request = jnp.sum(hot * (occ_flat % occ_dev + 1)[None, :], axis=1)
    return slot_of, half_of, request


def gather_kernel(half_ref, coef_ref, out_ref, sem):
    slots, rows = out_ref.shape[0], out_ref.shape[1]
    first = pl.multiple_of(lax.axis_index("aux") * rows, rows)

    def copy(s):
        half = jnp.maximum(half_ref[s], 0)
        return pltpu.make_async_copy(coef_ref.at[half, pl.ds(first, rows)], out_ref.at[s], sem)

    @pl.loop(0, slots)
    def _(s):
        copy(s).start()

    @pl.loop(0, slots)
    def _(s):
        copy(s).wait()


def rows_kernel(row_ref, coef_ref, ints_ref, out_ref):
    step = pl.program_id(0)
    for t in range(STEP_SLOTS):
        row = jnp.maximum(row_ref[step * STEP_SLOTS + t] - 1, 0)
        coef = coef_ref[:, t].reshape(-1, coef_ref.shape[-1])
        out_ref[t] = lax.dot_general(
            coef, ints_ref[row], (((0,), (0,)), ((), ())), preferred_element_type=jnp.float32
        ).astype(out_ref.dtype)


def coupling_kernel(slot_ref, rows_ref, out_ref):
    pairs = out_ref.shape[0]

    @pl.loop(0, pairs)
    def _(k):
        out_ref[k] = lax.dot_general(
            rows_ref[slot_ref[2 * k]],
            rows_ref[slot_ref[2 * k + 1]],
            (((1,), (1,)), ((), ())),
            preferred_element_type=jnp.float32,
        )


def gamma_kernel(slot_ref, occ_ref, count_ref, fock_ref, rows_ref, coupling_ref, energy_in_ref, out_ref, energy_ref):
    pairs, width, _ = coupling_ref.shape
    out_ref[...] = jnp.zeros_like(out_ref)
    row_id = lax.broadcasted_iota(jnp.int32, (width, width), 0)
    col_id = lax.broadcasted_iota(jnp.int32, (width, width), 1)

    @pl.loop(0, pairs)
    def _(k):
        slot_i, slot_j = slot_ref[2 * k], slot_ref[2 * k + 1]
        coupling = coupling_ref[k]
        by_col = jnp.broadcast_to(energy_in_ref[pl.ds(k, 1), :], (width, width))
        denom = by_col.T + by_col - fock_ref[occ_ref[2 * k]] - fock_ref[occ_ref[2 * k + 1]]
        inside = (row_id < count_ref[k]) & (col_id < count_ref[k])
        amplitude = jnp.where(inside, -coupling / denom, 0.0)
        mixed = 2.0 * amplitude - amplitude.T
        energy_ref[pl.ds(k, 1), :] = jnp.sum(coupling * mixed, axis=0, keepdims=True)
        weights = mixed.astype(jnp.bfloat16)
        out_ref[slot_i] = jnp.dot(weights, rows_ref[slot_j], preferred_element_type=jnp.float32).astype(out_ref.dtype)
        out_ref[slot_j] = lax.dot_general(
            weights, rows_ref[slot_i], (((0,), (0,)), ((), ())), preferred_element_type=jnp.float32
        ).astype(out_ref.dtype)


def grad_kernel(row_ref, coef_ref, gamma_ref, out_ref):
    step = pl.program_id(0)

    @pl.when(step == 0)
    def _():
        out_ref[...] = jnp.zeros_like(out_ref)

    for t in range(STEP_SLOTS):
        row = row_ref[step * STEP_SLOTS + t]

        @pl.when(row > 0)
        def _(t=t, row=row):
            coef = coef_ref[:, t].reshape(-1, coef_ref.shape[-1])
            term = jnp.dot(coef, gamma_ref[t], preferred_element_type=jnp.float32).astype(jnp.bfloat16)
            out_ref[row - 1] += term.astype(jnp.float32)


def params():
    return pltpu.CompilerParams(vmem_limit_bytes=VMEM_LIMIT)


def local(three_index, fock_diag, pair_occ, pno_count, pno_energy, pno_coef):
    groups = lax.axis_size("pair")
    planes = lax.axis_size("aux")
    occ_dev, width_dom, width_aux = three_index.shape
    pair_dev = pair_occ.shape[0]
    width_pno = pno_coef.shape[3]
    halves = 2 * pair_dev
    slots = groups * CAPACITY
    part = width_dom // planes
    smem = pl.BlockSpec(memory_space=pltpu.SMEM)
    vmem = pl.BlockSpec(memory_space=pltpu.VMEM)
    hbm = pl.BlockSpec(memory_space=pl.ANY)

    slot_of, half_of, request = plan_slots(pair_occ, groups, occ_dev)

    def exchange(x):
        y = x.reshape((groups, CAPACITY) + x.shape[1:])
        return lax.all_to_all(y, "pair", split_axis=0, concat_axis=0, tiled=True).reshape(x.shape)

    wanted = exchange(request)
    coef_part = pl.pallas_call(
        gather_kernel,
        name="gather_coef",
        out_shape=jax.ShapeDtypeStruct((slots, part, width_pno), jnp.bfloat16),
        in_specs=[smem, hbm],
        out_specs=hbm,
        scratch_shapes=[pltpu.SemaphoreType.DMA],
        compiler_params=params(),
    )(half_of, pno_coef.reshape(halves, width_dom, width_pno))
    coef = lax.all_gather(exchange(coef_part), "aux")

    steps = slots // STEP_SLOTS
    coef_spec = pl.BlockSpec((planes, STEP_SLOTS, part, width_pno), lambda s, r: (0, s, 0, 0))
    whole_spec = pl.BlockSpec((occ_dev, width_dom, width_aux), lambda s, r: (0, 0, 0))
    slot_spec = pl.BlockSpec((STEP_SLOTS, width_pno, width_aux), lambda s, r: (s, 0, 0))
    rows_out = pl.pallas_call(
        rows_kernel,
        name="project_rows",
        out_shape=jax.ShapeDtypeStruct((slots, width_pno, width_aux), jnp.bfloat16),
        grid_spec=pltpu.PrefetchScalarGridSpec(
            num_scalar_prefetch=1, grid=(steps,), in_specs=[coef_spec, whole_spec], out_specs=slot_spec
        ),
        compiler_params=params(),
    )(wanted, coef, three_index)
    rows = exchange(rows_out)

    partial_sum = pl.pallas_call(
        coupling_kernel,
        name="coupling_part",
        out_shape=jax.ShapeDtypeStruct((pair_dev, width_pno, width_pno), jnp.float32),
        in_specs=[smem, vmem],
        out_specs=vmem,
        compiler_params=params(),
    )(slot_of, rows)
    coupling = lax.psum(partial_sum, "aux")

    gamma_out, energy_cols = pl.pallas_call(
        gamma_kernel,
        name="weigh_rows",
        out_shape=(
            jax.ShapeDtypeStruct((slots, width_pno, width_aux), jnp.bfloat16),
            jax.ShapeDtypeStruct((pair_dev, width_pno), jnp.float32),
        ),
        in_specs=[smem, smem, smem, smem, vmem, vmem, vmem],
        out_specs=(vmem, vmem),
        compiler_params=params(),
    )(slot_of, pair_occ.reshape(halves), pno_count, fock_diag, rows, coupling, pno_energy)
    energy = jnp.sum(energy_cols, axis=1) / (width_pno * width_pno)
    gamma = exchange(gamma_out)

    grad = pl.pallas_call(
        grad_kernel,
        name="add_terms",
        out_shape=jax.ShapeDtypeStruct((occ_dev, width_dom, width_aux), jnp.float32),
        grid_spec=pltpu.PrefetchScalarGridSpec(
            num_scalar_prefetch=1, grid=(steps,), in_specs=[coef_spec, slot_spec], out_specs=whole_spec
        ),
        compiler_params=params(),
    )(wanted, coef, gamma)
    return energy, grad


def solution(mesh):
    placed = (
        P("pair", None, "aux"),
        P(),
        P("pair", None),
        P("pair"),
        P("pair", None),
        P("pair", None, None, None),
    )
    return jax.shard_map(
        local,
        mesh=mesh,
        in_specs=placed,
        out_specs=(P("pair"), P("pair", None, "aux")),
        check_vma=False,
    )
```

time: 717 us -> 434 us (0.61)
  waiting for transfers between devices: 478 us -> 195 us
  blocking collectives: 15.6 us -> 140 us
  local copies, waits for them, and re-layouts: 114 us -> 9.68 us
  Pallas kernels: 0 us -> 66.1 us
  matrix products: 54.5 us -> 0 us
  other arithmetic: 26.1 us -> 1.63 us
    all_to_all x2 -> x1, waiting for transfers between devices: 425 us -> 105 us  [exchange(): lax.all_to_all(y, 'pair', split_axis=0, concat_axis=0, tiled=True)]
    all_to_all x1 -> x3, blocking collectives: 15.6 us -> 140 us  [exchange(): lax.all_to_all(y, 'pair', split_axis=0, concat_axis=0, tiled=True)]
    pallas_call x0 -> x5, Pallas kernels: none -> 66.1 us  [the longest x1 20.9 us: local(): pl.pallas_call(grad_kernel, name='add_terms', out_shape=jax.ShapeDtypeStr...]
    dot_general x6 -> x0, matrix products: 54.5 us -> none  [the longest x1 16.8 us: local(): jnp.dot(occ_hot.astype(jnp.bfloat16), terms.reshape(slots, width_dom * wi...]
    scatter x2 -> x0, local copies, waits for them, and re-layouts: 42.6 us -> none  [the longest x1 41.8 us: local(): jnp.zeros((slots, width_dom, width_aux), jnp.bfloat16).at[slot_of]]
    all_gather x0 -> x1, waiting for transfers between devices: none -> 33.9 us  [local(): coef = lax.all_gather(exchange(coef_part), 'aux')]
    gather x4 -> x0, local copies, waits for them, and re-layouts: 24.5 us -> none  [the longest x1 13.3 us: local(): jnp.take(rows_back.reshape(slots, width_dom, width_aux), slot_of, axis=0)]
    convert_element_type x1 -> x0, local copies, waits for them, and re-layouts: 21.9 us -> none  [local(): dom_terms = jnp.einsum('hdp,hpq->hdq', coef_half, gamma, preferred_elemen...]
where the time goes in v1:
time: 434 us; the launch traced here: 433 us
  waiting for transfers between devices  195 us (45%)
  blocking collectives  140 us (32%)
  Pallas kernels  66.1 us (15%)
  between operations  14.1 us (3%)
  local copies, waits for them, and re-layouts  9.68 us (2%)
  starting transfers between devices  7.47 us (2%)
    all_to_all x3, blocking collectives, exchange(): lax.all_to_all(y, 'pair', split_axis=0, concat_axis=0, tiled=True)  140 us
    all_to_all x1, waiting for transfers between devices, exchange(): lax.all_to_all(y, 'pair', split_axis=0, concat_axis=0, tiled=True)  105 us
    psum x1, waiting for transfers between devices, local(): coupling = lax.psum(partial_sum, 'aux')  55.6 us
    all_gather x1, waiting for transfers between devices, local(): coef = lax.all_gather(exchange(coef_part), 'aux')  33.9 us
    pallas_call x1, Pallas kernels, local(): pl.pallas_call(grad_kernel, name='add_terms', out_shape=jax.ShapeDtypeStr...  20.9 us
    pallas_call x1, Pallas kernels, local(): pl.pallas_call(gamma_kernel, name='weigh_rows', out_shape=(jax.ShapeDtype...  19.3 us
    pallas_call x1, Pallas kernels, local(): pl.pallas_call(rows_kernel, name='project_rows', out_shape=jax.ShapeDtype...  12.2 us
    pallas_call x1, Pallas kernels, local(): pl.pallas_call(coupling_kernel, name='coupling_part', out_shape=jax.Shape...  10.6 us
  transfers between devices with their start and end apart: 3, of which 3 were waited for; matrix products, arithmetic and copies ran while one was open for 0% of the time, Pallas kernels for 0%

profile of v1, /device:TPU:0, one launch (start us, length us, event | category | flops | bytes accessed | tf_op | source)
XLA Modules:
  0.0 433.4 jit_solution(1294326974433848054)
XLA Ops:
  7.2 0.0 all-gather.2.cloned.1.call-start
  7.2 0.8 copy.12
  8.0 0.1 reshape.129.occ_ref
  8.1 0.2 convert_reduce_fusion
  8.3 0.1 select_reduce_fusion
  8.4 0.0 copy-start.2
  8.4 2.1 copy-done.2
  10.6 3.0 gather_coef.1
  13.6 25.7 %all_to_all.24 = bf16[32,2,64,128]{3,2,1,0:T(8,128)(2,1)} all-to-all(bf16[32,2,64,128]{3,2,1,0:T(8,128)(2,1)S(1)} %bitcast.8), channel_id=1, replica_groups=mesh['aux'=4,'pair'=32] {'pair'}, dimensions={0} | all-to-all | bytes 2097152 | tf_op jit(solution)/shard_map/all_to_all | solution.py:130
  39.3 0.0 all-gather.2.cloned.1.call-update
  39.3 0.0 all-reduce.2.cloned.1.call-start
  39.3 0.1 all_to_all.15
  39.4 10.7 %all_to_all.25 = s32[32,1,2]{2,1,0:T(1,128)S(1)} all-to-all(s32[32,1,2]{2,1,0:T(1,128)S(1)} %bitcast.15), channel_id=1, replica_groups=mesh['aux'=4,'pair'=32] {'pair'}, dimensions={0} | all-to-all | bytes 512 | tf_op jit(solution)/shard_map/all_to_all | solution.py:130
  50.1 0.5 broadcast.150
  50.7 0.7 reduce.3
  51.4 0.1 reshape.130.row_ref
  51.5 33.9 %all-gather.2.cloned.1.call-done.coef_ref = bf16[4,64,64,128]{3,2,1,0:T(8,128)(2,1)} async-done(((bf16[1,64,64,128]{3,2,1,0:T(8,128)(2,1)}), bf16[4,64,64,128]{3,2,1,0:T(8,128)(2,1)}) %all-gather.2.cloned.1.call-update) | async-done | bytes 4194320 | tf_op jit(solution)/shard_map/all_gather | solution.py:142
  85.3 0.0 copy-start
  85.3 2.2 copy-done
  87.5 12.2 %project_rows.1 = bf16[64,128,512]{2,1,0:T(8,128)(2,1)} custom-call(s32[64]{0:T(128)S(1)} %reshape.130.row_ref, bf16[4,64,64,128]{3,2,1,0:T(8,128)(2,1)S(1)} %copy-done, bf16[16,256,512]{2,1,0:T(8,128)(2,1)} %ints_ref.1), custom_call_target="tpu_custom_call" | custom-call | tf_op jit(solution)/shard_map/project_rows/pallas_call | solution.py:148
  99.7 103.4 %all_to_all.26 = bf16[32,2,128,512]{3,2,1,0:T(8,128)(2,1)} all-to-all(bf16[32,2,128,512]{3,2,1,0:T(8,128)(2,1)} %bitcast.12), channel_id=1, replica_groups=mesh['aux'=4,'pair'=32] {'pair'}, dimensions={0} | all-to-all | bytes 16777216 | tf_op jit(solution)/shard_map/all_to_all | solution.py:130
  203.1 0.0 copy-start.4
  203.1 0.0 copy-start.5
  203.1 0.0 copy-start.6
  203.1 10.6 %coupling_part.1 = f32[31,128,128]{2,1,0:T(8,128)} custom-call(s32[62]{0:T(128)S(1)} %multiply_add_fusion.slot_ref, bf16[64,128,512]{2,1,0:T(8,128)(2,1)} %bitcast.10), custom_call_target="tpu_custom_call" | custom-call | tf_op jit(solution)/shard_map/coupling_part/pallas_call | solution.py:159
  213.7 0.0 all-reduce.2.cloned.1.call-update
  213.7 55.6 %all-reduce.2.cloned.1.call-done.coupling_ref = f32[31,128,128]{2,1,0:T(8,128)} async-done(((f32[31,128,128]{2,1,0:T(8,128)}), f32[31,128,128]{2,1,0:T(8,128)}) %all-reduce.2.cloned.1.call-update) | async-done | bytes 2031632 | tf_op jit(solution)/shard_map/psum | solution.py:167
  269.3 0.0 copy-done.4
  269.3 0.0 copy-done.5
  269.3 0.0 copy-done.6
  269.3 0.0 copy-start.3
  269.3 1.6 copy-done.3
  270.9 19.3 %weigh_rows.1 = (bf16[64,128,512]{2,1,0:T(8,128)(2,1)}, f32[31,128]{1,0:T(8,128)S(1)}) custom-call(s32[62]{0:T(128)S(1)} %multiply_add_fusion.slot_ref, s32[62]{0:T(128)S(1)} %reshape.129.occ_ref, s32[31]{0:T(128)S(1)} %copy-done.6, f32[512]{0:T(512)S(1)} %copy-done.5, bf16[64,128,512]{2,1,0:T(8,128)(2,1)} %bitcast.11, f32[31,128,128]{2,1,0:T(8,128)S(1)} %copy-done.3, ...), custom_call_target="tpu_custom_call" | custom-call | tf_op jit(solution)/shard_map/weigh_rows/pallas_call | solution.py:169
  290.2 7.4 %all-to-all-start.3 = ((bf16[32,2,128,512]{3,2,1,0:T(8,128)(2,1)}), bf16[32,2,128,512]{3,2,1,0:T(8,128)(2,1)}, u32[]{:S(2)}, u32[]{:S(2)}) async-start(bf16[32,2,128,512]{3,2,1,0:T(8,128)(2,1)} %bitcast.13), calls=%async_computation.3 | async-start | bytes 16777216 | tf_op jit(solution)/shard_map/all_to_all | solution.py:130
  297.6 0.1 reduce_sum.39
  297.7 0.5 broadcast_multiply_fusion
  298.2 105.2 %all-to-all-done.3 = bf16[32,2,128,512]{3,2,1,0:T(8,128)(2,1)} async-done(((bf16[32,2,128,512]{3,2,1,0:T(8,128)(2,1)}), bf16[32,2,128,512]{3,2,1,0:T(8,128)(2,1)}, u32[]{:S(2)}, u32[]{:S(2)}) %all-to-all-start.3) | async-done | bytes 8388640 | tf_op jit(solution)/shard_map/all_to_all | solution.py:130
  403.5 0.0 copy-start.1
  403.5 2.2 copy-done.1
  405.7 20.9 %add_terms.1 = f32[16,256,512]{2,1,0:T(8,128)} custom-call(s32[64]{0:T(128)S(1)} %reshape.130.row_ref, bf16[4,64,64,128]{3,2,1,0:T(8,128)(2,1)S(1)} %copy-done.1, bf16[64,128,512]{2,1,0:T(8,128)(2,1)} %bitcast.7.gamma_ref), custom_call_target="tpu_custom_call" | custom-call | tf_op jit(solution)/shard_map/add_terms/pallas_call | solution.py:183
  (3 shorter events, 0.0 us)
Async XLA Ops:
  7.2 78.2 %all-gather.2.cloned.1.call-start = ((), (), s32[]{:S(2)}) async-start(), calls=%async_computation.4 | async-start | bytes 5242880 | tf_op jit(solution)/shard_map/all_gather | solution.py:142
  8.4 2.2 copy-start.2
  39.3 230.0 %all-reduce.2.cloned.1.call-start = ((), (), s32[]{:S(2)}) async-start(), calls=%async_computation.5 | async-start | bytes 4063232 | tf_op jit(solution)/shard_map/psum | solution.py:167
  85.3 2.2 copy-start
  203.1 66.2 %copy-start.4 = (f32[31,128]{1,0:T(8,128)S(1)}, f32[31,128]{1,0:T(8,128)}, u32[]{:S(2)}) copy-start(f32[31,128]{1,0:T(8,128)} %energy_in_ref.1) | copy-start | bytes 47620
  203.1 66.2 %copy-start.5 = (f32[512]{0:T(512)S(1)}, f32[512]{0:T(512)}, u32[]{:S(2)}) copy-start(f32[512]{0:T(512)} %fock_ref.1) | copy-start | bytes 6148
  203.1 66.2 %copy-start.6 = (s32[31]{0:T(128)S(1)}, s32[31]{0:T(128)}, u32[]{:S(2)}) copy-start(s32[31]{0:T(128)} %count_ref.1) | copy-start | bytes 376
  269.3 1.6 copy-start.3
  290.2 113.3 %all-to-all-start.3 = ((bf16[32,2,128,512]{3,2,1,0:T(8,128)(2,1)}), bf16[32,2,128,512]{3,2,1,0:T(8,128)(2,1)}, u32[]{:S(2)}, u32[]{:S(2)}) async-start(bf16[32,2,128,512]{3,2,1,0:T(8,128)(2,1)} %bitcast.13), calls=%async_computation.3 | async-start | bytes 16777216 | tf_op jit(solution)/shard_map/all_to_all | solution.py:130
  403.5 2.2 copy-start.1
Sparse Core Ops, SparseCore 0:
  39.4 45.8 all-gather.1
  213.8 55.4 all-reduce.1

commit v2 on v1

--- a/solution.py
+++ b/solution.py
@@ -9,6 +9,7 @@
 
 CAPACITY = 2
 STEP_SLOTS = 4
+MESH = pl.DeviceIdType.MESH
 VMEM_LIMIT = 48 << 20
 
 
@@ -43,14 +44,103 @@
         copy(s).wait()
 
 
-def rows_kernel(row_ref, coef_ref, ints_ref, out_ref):
-    step = pl.program_id(0)
-    for t in range(STEP_SLOTS):
-        row = jnp.maximum(row_ref[step * STEP_SLOTS + t] - 1, 0)
-        coef = coef_ref[:, t].reshape(-1, coef_ref.shape[-1])
-        out_ref[t] = lax.dot_general(
-            coef, ints_ref[row], (((0,), (0,)), ((), ())), preferred_element_type=jnp.float32
-        ).astype(out_ref.dtype)
+def place():
+    me = lax.axis_index("pair")
+    return me // 8, lax.rem(me // 2, 4), lax.rem(me, 2)
+
+
+def device(z, y, core):
+    return {"pair": (z * 4 + y) * 2 + core}
+
+
+def greet():
+    z, y, core = place()
+    barrier = pltpu.get_barrier_semaphore()
+    peers = [device(z, y, 1 - core)]
+    for d in (1, 2, 3):
+        for c in (core, 1 - core):
+            peers += [device(lax.rem(z + d, 4), y, c), device(z, lax.rem(y + d, 4), c)]
+    for peer in peers:
+        pl.semaphore_signal(barrier, inc=1, device_id=peer, device_id_type=MESH)
+    pl.semaphore_wait(barrier, len(peers))
+
+
+def exchange_in_kernel(produce, send, transit, recv, hop_send, hop_recv, last_send, last_recv):
+    z, y, core = place()
+    here, across = (z, y), (y, z)
+    hops = {}
+    for d in (1, 3, 2, 0):
+        for way in (0, 1):
+            group = lax.rem(here[way] + d, 4)
+            produce(way, group)
+            if d:
+                n = way * 3 + d - 1
+                hops[way, d] = pltpu.make_async_remote_copy(
+                    src_ref=send.at[way, group],
+                    dst_ref=transit.at[way, here[way]],
+                    send_sem=hop_send.at[n],
+                    recv_sem=hop_recv.at[n],
+                    device_id=device(group, y, core) if way == 0 else device(z, group, core),
+                    device_id_type=MESH,
+                )
+                hops[way, d].start()
+    last = []
+    for ds in (0, 1, 3, 2):
+        for way in (0, 1):
+            source = lax.rem(here[way] + 4 - ds, 4)
+            if ds:
+                hops[way, ds].wait_recv()
+            origin = (source * 4 + y) * 2 + core if way == 0 else (z * 4 + source) * 2 + core
+            for d in (1, 3, 2, 0):
+                for dc in (0, 1):
+                    to, to_core = lax.rem(across[way] + d, 4), lax.rem(core + dc, 2)
+                    block = (transit if ds else send).at[way, source, to * 2 + to_core]
+                    n = ((way * 4 + ds) * 4 + d) * 2 + dc
+                    if d == 0 and dc == 0:
+                        copy = pltpu.make_async_copy(block, recv.at[origin, way], last_send.at[n])
+                    else:
+                        copy = pltpu.make_async_remote_copy(
+                            src_ref=block,
+                            dst_ref=recv.at[origin, way],
+                            send_sem=last_send.at[n],
+                            recv_sem=last_recv.at[n],
+                            device_id=device(z, to, to_core) if way == 0 else device(to, y, to_core),
+                            device_id_type=MESH,
+                        )
+                    copy.start()
+                    last.append(copy)
+    for hop in hops.values():
+        hop.wait_send()
+    for copy in last:
+        copy.wait()
+
+
+def exchange_scratch(shape):
+    return [
+        pltpu.VMEM((2, 4, 8) + shape, jnp.bfloat16),
+        pltpu.VMEM((2, 4, 8) + shape, jnp.bfloat16),
+        pltpu.SemaphoreType.DMA((6,)),
+        pltpu.SemaphoreType.DMA((6,)),
+        pltpu.SemaphoreType.DMA((64,)),
+        pltpu.SemaphoreType.DMA((64,)),
+    ]
+
+
+def rows_kernel(row_ref, coef_ref, ints_ref, recv_ref, send_ref, transit_ref, *sems):
+    greet()
+
+    def produce(way, group):
+        @pl.loop(0, 8)
+        def _(t):
+            owner = group * 8 + t if way == 0 else (t // 2 * 4 + group) * 2 + lax.rem(t, 2)
+            slot = owner * CAPACITY + way
+            coef = coef_ref[:, slot].reshape(-1, coef_ref.shape[-1])
+            row = jnp.maximum(row_ref[slot] - 1, 0)
+            send_ref[way, group, t] = lax.dot_general(
+                coef, ints_ref[row], (((0,), (0,)), ((), ())), preferred_element_type=jnp.float32
+            ).astype(send_ref.dtype)
+
+    exchange_in_kernel(produce, send_ref, transit_ref, recv_ref, *sems)
 
 
 def coupling_kernel(slot_ref, rows_ref, out_ref):
@@ -106,8 +196,10 @@
             out_ref[row - 1] += term.astype(jnp.float32)
 
 
-def params():
-    return pltpu.CompilerParams(vmem_limit_bytes=VMEM_LIMIT)
+def params(collective_id=None):
+    return pltpu.CompilerParams(
+        vmem_limit_bytes=VMEM_LIMIT, collective_id=collective_id, has_side_effects=collective_id is not None
+    )
 
 
 def local(three_index, fock_diag, pair_occ, pno_count, pno_energy, pno_coef):
@@ -145,16 +237,15 @@
     coef_spec = pl.BlockSpec((planes, STEP_SLOTS, part, width_pno), lambda s, r: (0, s, 0, 0))
     whole_spec = pl.BlockSpec((occ_dev, width_dom, width_aux), lambda s, r: (0, 0, 0))
     slot_spec = pl.BlockSpec((STEP_SLOTS, width_pno, width_aux), lambda s, r: (s, 0, 0))
-    rows_out = pl.pallas_call(
+    rows = pl.pallas_call(
         rows_kernel,
-        name="project_rows",
-        out_shape=jax.ShapeDtypeStruct((slots, width_pno, width_aux), jnp.bfloat16),
-        grid_spec=pltpu.PrefetchScalarGridSpec(
-            num_scalar_prefetch=1, grid=(steps,), in_specs=[coef_spec, whole_spec], out_specs=slot_spec
-        ),
-        compiler_params=params(),
-    )(wanted, coef, three_index)
-    rows = exchange(rows_out)
+        name="project_and_return_rows",
+        out_shape=jax.ShapeDtypeStruct((groups, CAPACITY, width_pno, width_aux), jnp.bfloat16),
+        in_specs=[smem, vmem, vmem],
+        out_specs=hbm,
+        scratch_shapes=exchange_scratch((width_pno, width_aux)),
+        compiler_params=params(1),
+    )(wanted, coef, three_index).reshape(slots, width_pno, width_aux)
 
     partial_sum = pl.pallas_call(
         coupling_kernel,

time: 434 us -> 425 us (0.979)
  blocking collectives: 140 us -> 36.4 us
  Pallas kernels: 66.1 us -> 158 us
    all_to_all x3 -> x2, blocking collectives: 140 us -> 36.4 us  [exchange(): lax.all_to_all(y, 'pair', split_axis=0, concat_axis=0, tiled=True)]
    pallas_call x1, Pallas kernels: 12.2 us -> 104 us  [local(): pl.pallas_call(rows_kernel, name='project_and_return_rows', out_shape=jax...]
where the time goes in v2:
time: 425 us
  waiting for transfers between devices  198 us (47%)
  Pallas kernels  158 us (37%)
  blocking collectives  36.4 us (9%)
  between operations  14.2 us (3%)
  local copies, waits for them, and re-layouts  9.69 us (2%)
  starting transfers between devices  7.48 us (2%)
    all_to_all x1, waiting for transfers between devices, exchange(): lax.all_to_all(y, 'pair', split_axis=0, concat_axis=0, tiled=True)  105 us
    pallas_call x1, Pallas kernels, local(): pl.pallas_call(rows_kernel, name='project_and_return_rows', out_shape=jax...  104 us
    psum x1, waiting for transfers between devices, local(): coupling = lax.psum(partial_sum, 'aux')  58.6 us
    all_to_all x2, blocking collectives, exchange(): lax.all_to_all(y, 'pair', split_axis=0, concat_axis=0, tiled=True)  36.4 us
    all_gather x1, waiting for transfers between devices, local(): coef = lax.all_gather(exchange(coef_part), 'aux')  33.9 us
    pallas_call x1, Pallas kernels, local(): pl.pallas_call(grad_kernel, name='add_terms', out_shape=jax.ShapeDtypeStr...  20.8 us
    pallas_call x1, Pallas kernels, local(): pl.pallas_call(gamma_kernel, name='weigh_rows', out_shape=(jax.ShapeDtype...  19.3 us
    pallas_call x1, Pallas kernels, local(): pl.pallas_call(coupling_kernel, name='coupling_part', out_shape=jax.Shape...  10.6 us
  transfers between devices with their start and end apart: 3, of which 3 were waited for; matrix products, arithmetic and copies ran while one was open for 0% of the time, Pallas kernels for 0%

profile of v2, /device:TPU:0, one launch (start us, length us, event | category | flops | bytes accessed | tf_op | source)
XLA Modules:
  0.0 424.6 jit_solution(4441762629435731392)
XLA Ops:
  7.2 0.0 all-gather.2.cloned.1.call-start
  7.2 0.8 copy.12
  8.0 0.1 reshape.126.occ_ref
  8.1 0.2 convert_reduce_fusion
  8.3 0.1 select_reduce_fusion
  8.4 0.0 copy-start.2
  8.4 2.1 copy-done.2
  10.6 3.0 gather_coef.1
  13.6 25.7 %all_to_all.19 = bf16[32,2,64,128]{3,2,1,0:T(8,128)(2,1)} all-to-all(bf16[32,2,64,128]{3,2,1,0:T(8,128)(2,1)S(1)} %bitcast.7), channel_id=1, replica_groups=mesh['aux'=4,'pair'=32] {'pair'}, dimensions={0} | all-to-all | bytes 2097152 | tf_op jit(solution)/shard_map/all_to_all | solution.py:222
  39.3 0.0 all-gather.2.cloned.1.call-update
  39.3 0.0 all-reduce.2.cloned.1.call-start
  39.3 0.1 all_to_all.12
  39.4 10.7 %all_to_all.20 = s32[32,1,2]{2,1,0:T(1,128)S(1)} all-to-all(s32[32,1,2]{2,1,0:T(1,128)S(1)} %bitcast.13), channel_id=1, replica_groups=mesh['aux'=4,'pair'=32] {'pair'}, dimensions={0} | all-to-all | bytes 512 | tf_op jit(solution)/shard_map/all_to_all | solution.py:222
  50.1 0.5 broadcast.150
  50.7 0.7 reduce.3
  51.4 0.1 reshape.127.row_ref
  51.5 33.9 %all-gather.2.cloned.1.call-done.coef_ref = bf16[4,64,64,128]{3,2,1,0:T(8,128)(2,1)} async-done(((bf16[1,64,64,128]{3,2,1,0:T(8,128)(2,1)}), bf16[4,64,64,128]{3,2,1,0:T(8,128)(2,1)}) %all-gather.2.cloned.1.call-update) | async-done | bytes 4194320 | tf_op jit(solution)/shard_map/all_gather | solution.py:234
  85.3 0.0 copy-start
  85.3 2.2 copy-done
  87.5 103.8 %project_and_return_rows.1 = bf16[32,2,128,512]{3,2,1,0:T(8,128)(2,1)} custom-call(s32[64]{0:T(128)S(1)} %reshape.127.row_ref, bf16[4,64,64,128]{3,2,1,0:T(8,128)(2,1)S(1)} %copy-done, bf16[16,256,512]{2,1,0:T(8,128)(2,1)} %ints_ref.1), custom_call_target="tpu_custom_call" | custom-call | tf_op jit(solution)/shard_map/project_and_return_rows/pallas_call | solution.py:240
  191.3 0.0 copy-start.4
  191.3 0.0 copy-start.5
  191.4 0.0 copy-start.6
  191.4 10.6 %coupling_part.1 = f32[31,128,128]{2,1,0:T(8,128)} custom-call(s32[62]{0:T(128)S(1)} %multiply_add_fusion.slot_ref, bf16[64,128,512]{2,1,0:T(8,128)(2,1)} %bitcast.9), custom_call_target="tpu_custom_call" | custom-call | tf_op jit(solution)/shard_map/coupling_part/pallas_call | solution.py:250
  201.9 0.0 all-reduce.2.cloned.1.call-update
  202.0 58.6 %all-reduce.2.cloned.1.call-done.coupling_ref = f32[31,128,128]{2,1,0:T(8,128)} async-done(((f32[31,128,128]{2,1,0:T(8,128)}), f32[31,128,128]{2,1,0:T(8,128)}) %all-reduce.2.cloned.1.call-update) | async-done | bytes 2031632 | tf_op jit(solution)/shard_map/psum | solution.py:258
  260.6 0.0 copy-done.4
  260.6 0.0 copy-done.5
  260.6 0.0 copy-done.6
  260.6 0.0 copy-start.3
  260.6 1.6 copy-done.3
  262.1 19.3 %weigh_rows.1 = (bf16[64,128,512]{2,1,0:T(8,128)(2,1)}, f32[31,128]{1,0:T(8,128)S(1)}) custom-call(s32[62]{0:T(128)S(1)} %multiply_add_fusion.slot_ref, s32[62]{0:T(128)S(1)} %reshape.126.occ_ref, s32[31]{0:T(128)S(1)} %copy-done.6, f32[512]{0:T(512)S(1)} %copy-done.5, bf16[64,128,512]{2,1,0:T(8,128)(2,1)} %bitcast.10, f32[31,128,128]{2,1,0:T(8,128)S(1)} %copy-done.3, ...), custom_call_target="tpu_custom_call" | custom-call | tf_op jit(solution)/shard_map/weigh_rows/pallas_call | solution.py:260
  281.5 7.4 %all-to-all-start.2 = ((bf16[32,2,128,512]{3,2,1,0:T(8,128)(2,1)}), bf16[32,2,128,512]{3,2,1,0:T(8,128)(2,1)}, u32[]{:S(2)}, u32[]{:S(2)}) async-start(bf16[32,2,128,512]{3,2,1,0:T(8,128)(2,1)} %bitcast.11), calls=%async_computation.2 | async-start | bytes 16777216 | tf_op jit(solution)/shard_map/all_to_all | solution.py:222
  288.9 0.1 reduce_sum.39
  289.0 0.5 broadcast_multiply_fusion
  289.5 105.2 %all-to-all-done.2 = bf16[32,2,128,512]{3,2,1,0:T(8,128)(2,1)} async-done(((bf16[32,2,128,512]{3,2,1,0:T(8,128)(2,1)}), bf16[32,2,128,512]{3,2,1,0:T(8,128)(2,1)}, u32[]{:S(2)}, u32[]{:S(2)}) %all-to-all-start.2) | async-done | bytes 8388640 | tf_op jit(solution)/shard_map/all_to_all | solution.py:222
  394.7 0.0 copy-start.1
  394.8 2.2 copy-done.1
  396.9 20.8 %add_terms.1 = f32[16,256,512]{2,1,0:T(8,128)} custom-call(s32[64]{0:T(128)S(1)} %reshape.127.row_ref, bf16[4,64,64,128]{3,2,1,0:T(8,128)(2,1)S(1)} %copy-done.1, bf16[64,128,512]{2,1,0:T(8,128)(2,1)} %bitcast.6.gamma_ref), custom_call_target="tpu_custom_call" | custom-call | tf_op jit(solution)/shard_map/add_terms/pallas_call | solution.py:274
  (3 shorter events, 0.0 us)
Async XLA Ops:
  7.2 78.2 %all-gather.2.cloned.1.call-start = ((), (), s32[]{:S(2)}) async-start(), calls=%async_computation.3 | async-start | bytes 5242880 | tf_op jit(solution)/shard_map/all_gather | solution.py:234
  8.4 2.2 copy-start.2
  39.3 221.3 %all-reduce.2.cloned.1.call-start = ((), (), s32[]{:S(2)}) async-start(), calls=%async_computation.4 | async-start | bytes 4063232 | tf_op jit(solution)/shard_map/psum | solution.py:258
  85.3 2.2 copy-start
  191.3 69.2 %copy-start.4 = (f32[31,128]{1,0:T(8,128)S(1)}, f32[31,128]{1,0:T(8,128)}, u32[]{:S(2)}) copy-start(f32[31,128]{1,0:T(8,128)} %energy_in_ref.1) | copy-start | bytes 47620
  191.3 69.2 %copy-start.5 = (f32[512]{0:T(512)S(1)}, f32[512]{0:T(512)}, u32[]{:S(2)}) copy-start(f32[512]{0:T(512)} %fock_ref.1) | copy-start | bytes 6148
  191.4 69.2 %copy-start.6 = (s32[31]{0:T(128)S(1)}, s32[31]{0:T(128)}, u32[]{:S(2)}) copy-start(s32[31]{0:T(128)} %count_ref.1) | copy-start | bytes 376
  260.6 1.6 copy-start.3
  281.5 113.3 %all-to-all-start.2 = ((bf16[32,2,128,512]{3,2,1,0:T(8,128)(2,1)}), bf16[32,2,128,512]{3,2,1,0:T(8,128)(2,1)}, u32[]{:S(2)}, u32[]{:S(2)}) async-start(bf16[32,2,128,512]{3,2,1,0:T(8,128)(2,1)} %bitcast.11), calls=%async_computation.2 | async-start | bytes 16777216 | tf_op jit(solution)/shard_map/all_to_all | solution.py:222
  394.7 2.2 copy-start.1
Sparse Core Ops, SparseCore 0:
  39.4 45.8 all-gather.1
  202.1 58.4 all-reduce.1

commit v3 on v2

v3 whole, which is shorter than its diff:
```python
import functools

import jax
import jax.numpy as jnp
from jax import lax
from jax.experimental import pallas as pl
from jax.experimental.pallas import tpu as pltpu
from jax.sharding import PartitionSpec as P

CAPACITY = 2
MESH = pl.DeviceIdType.MESH
GROUP_ORDER = (1, 3, 2, 0)
VMEM_LIMIT = 48 << 20


def plan_slots(pair_occ, groups, occ_dev):
    occ_flat = pair_occ.reshape(-1)
    halves = occ_flat.shape[0]
    owner = occ_flat // occ_dev
    half_ids = jnp.arange(halves, dtype=jnp.int32)
    earlier = (owner[None, :] == owner[:, None]) & (half_ids[None, :] < half_ids[:, None])
    rank = jnp.sum(earlier.astype(jnp.int32), axis=1)
    slot_of = owner * CAPACITY + rank
    hot = (slot_of[None, :] == jnp.arange(groups * CAPACITY, dtype=jnp.int32)[:, None]).astype(jnp.int32)
    half_of = jnp.sum(hot * (half_ids + 1)[None, :], axis=1) - 1
    request = jnp.sum(hot * (occ_flat % occ_dev + 1)[None, :], axis=1)
    partner = jnp.sum(hot * slot_of.reshape(-1, 2)[:, ::-1].reshape(-1)[None, :], axis=1)
    return slot_of, half_of, request, partner


def place():
    me = lax.axis_index("pair")
    return me // 8, lax.rem(me // 2, 4), lax.rem(me, 2)


def device(z, y, core):
    return {"pair": (z * 4 + y) * 2 + core}


def plane(d):
    return {"aux": lax.rem(lax.axis_index("aux") + d, 4)}


def greet():
    z, y, core = place()
    barrier = pltpu.get_barrier_semaphore()
    peers = [device(z, y, 1 - core)]
    for d in (1, 2, 3):
        peers.append(plane(d))
        for c in (core, 1 - core):
            peers += [device(lax.rem(z + d, 4), y, c), device(z, lax.rem(y + d, 4), c)]
    for peer in peers:
        pl.semaphore_signal(barrier, inc=1, device_id=peer, device_id_type=MESH)
    pl.semaphore_wait(barrier, len(peers))


def start_exchange(produce, deliver, send, transit, hop_send, hop_recv, last_send, last_recv):
    z, y, core = place()
    here, across = (z, y), (y, z)
    hops, last = {}, {}
    for d in GROUP_ORDER:
        for way in (0, 1):
            group = lax.rem(here[way] + d, 4)
            produce(way, d, group)
            if d:
                n = way * 3 + d - 1
                hops[way, d] = pltpu.make_async_remote_copy(
                    src_ref=send.at[way, group],
                    dst_ref=transit.at[way, here[way]],
                    send_sem=hop_send.at[n],
                    recv_sem=hop_recv.at[n],
                    device_id=device(group, y, core) if way == 0 else device(z, group, core),
                    device_id_type=MESH,
                )
                hops[way, d].start()
    for ds in (0, 1, 3, 2):
        for way in (0, 1):
            source = lax.rem(here[way] + 4 - ds, 4)
            if ds:
                hops[way, ds].wait_recv()
            last[way, ds] = []
            for d in GROUP_ORDER:
                for dc in (0, 1):
                    to, to_core = lax.rem(across[way] + d, 4), lax.rem(core + dc, 2)
                    block = (transit if ds else send).at[way, source, to * 2 + to_core]
                    dst = deliver(way, source, across[way] * 2 + core)
                    n = ((way * 4 + ds) * 4 + d) * 2 + dc
                    if d == 0 and dc == 0:
                        copy = pltpu.make_async_copy(block, dst, last_send.at[n])
                    else:
                        copy = pltpu.make_async_remote_copy(
                            src_ref=block,
                            dst_ref=dst,
                            send_sem=last_send.at[n],
                            recv_sem=last_recv.at[n],
                            device_id=device(z, to, to_core) if way == 0 else device(to, y, to_core),
                            device_id_type=MESH,
                        )
                    copy.start()
                    last[way, ds].append((copy, d > 0 or dc > 0))
    return hops, last


def wait_arrivals(copies):
    for copy, remote in copies:
        if remote:
            copy.wait_recv()
        else:
            copy.wait()


def wait_sends(hops, last):
    for hop in hops.values():
        hop.wait_send()
    for copies in last.values():
        for copy, remote in copies:
            if remote:
                copy.wait_send()


def exchange_in_kernel(produce, deliver, *scratch):
    hops, last = start_exchange(produce, deliver, *scratch)
    for copies in last.values():
        wait_arrivals(copies)
    wait_sends(hops, last)


def exchange_scratch(shape):
    return [
        pltpu.VMEM((2, 4, 8) + shape, jnp.bfloat16),
        pltpu.VMEM((2, 4, 8) + shape, jnp.bfloat16),
        pltpu.SemaphoreType.DMA((6,)),
        pltpu.SemaphoreType.DMA((6,)),
        pltpu.SemaphoreType.DMA((64,)),
        pltpu.SemaphoreType.DMA((64,)),
    ]


def slot_at(way, group, t):
    owner = group * 8 + t if way == 0 else (t // 2 * 4 + group) * 2 + lax.rem(t, 2)
    return owner * CAPACITY + way


def start_tables(table, hop_send, hop_recv, last_send, last_recv):
    z, y, core = place()
    mine = y * 2 + core
    hops, last = [], []
    for d in (1, 3, 2):
        hops.append(
            pltpu.make_async_remote_copy(
                src_ref=table.at[mine, z],
                dst_ref=table.at[mine, z],
                send_sem=hop_send.at[d - 1],
                recv_sem=hop_recv.at[d - 1],
                device_id=device(lax.rem(z + d, 4), y, core),
                device_id_type=MESH,
            )
        )
        hops[-1].start()
    for copy in hops:
        copy.wait()
    for d in GROUP_ORDER:
        for dc in (0, 1):
            if d or dc:
                n = d * 2 + dc
                last.append(
                    pltpu.make_async_remote_copy(
                        src_ref=table.at[mine],
                        dst_ref=table.at[mine],
                        send_sem=last_send.at[n],
                        recv_sem=last_recv.at[n],
                        device_id=device(z, lax.rem(y + d, 4), lax.rem(core + dc, 2)),
                        device_id_type=MESH,
                    )
                )
                last[-1].start()
    return last


def fetch_kernel(
    half_ref, request_ref, own_coef_ref, ints_hbm_ref,
    recv_ref, coef_ref, wanted_ref,
    ints_ref, ints_sem, table_ref, table_smem, table_sem,
    table_hop_send, table_hop_recv, table_last_send, table_last_recv,
    coef_send_ref, coef_transit_ref, coef_hop_send, coef_hop_recv, coef_last_send, coef_last_recv,
    plane_send, plane_recv,
    send_ref, transit_ref, *sems,
):
    z, y, core = place()
    here = (z, y)
    mine = lax.axis_index("aux")
    rows = coef_ref.shape[4]
    first = pl.multiple_of(mine * rows, rows)
    load = pltpu.make_async_copy(ints_hbm_ref, ints_ref, ints_sem)
    load.start()
    table_ref[y * 2 + core, z] = request_ref[...]
    greet()

    def pick(way, d, group):
        @pl.loop(0, 8)
        def _(t):
            coef_send_ref[way, group, t] = own_coef_ref[half_ref[slot_at(way, group, t)], pl.ds(first, rows), :]

    coef_hops, coef_last = start_exchange(
        pick,
        lambda way, group, t: coef_ref.at[mine, way, group, t],
        coef_send_ref, coef_transit_ref, coef_hop_send, coef_hop_recv, coef_last_send, coef_last_recv,
    )
    tables = start_tables(table_ref, table_hop_send, table_hop_recv, table_last_send, table_last_recv)

    batches = [(way, (4 - d) % 4) for d in GROUP_ORDER for way in (0, 1)]
    shared = {}

    def share(way, ds):
        wait_arrivals(coef_last[way, ds])
        block = coef_ref.at[mine, way, lax.rem(here[way] + 4 - ds, 4)]
        shared[way, ds] = []
        for d in (2, 1, 3):
            n = (way * 4 + ds) * 3 + d - 1
            copy = pltpu.make_async_remote_copy(
                src_ref=block,
                dst_ref=block,
                send_sem=plane_send.at[n],
                recv_sem=plane_recv.at[n],
                device_id=plane(d),
                device_id_type=MESH,
            )
            copy.start()
            shared[way, ds].append(copy)

    for batch in batches[:2]:
        share(*batch)
    for copy in tables:
        copy.wait()
    to_smem = pltpu.make_async_copy(table_ref, table_smem, table_sem)
    to_smem.start()
    to_smem.wait()
    load.wait()
    me = lax.axis_index("pair")

    def produce(way, d, group):
        place_in_order = batches.index((way, (4 - d) % 4))
        if place_in_order + 2 < len(batches):
            share(*batches[place_in_order + 2])
        for copy in shared[way, (4 - d) % 4]:
            copy.wait_recv()

        @pl.loop(0, 8)
        def _(t):
            slot = slot_at(way, group, t)
            owner = slot // CAPACITY
            wanted = table_smem[lax.rem(owner, 8), owner // 8, 0, me * CAPACITY + way]
            wanted_ref[slot] = wanted
            coef = coef_ref[:, way, group, t].reshape(-1, coef_ref.shape[-1])
            send_ref[way, group, t] = lax.dot_general(
                coef, ints_ref[jnp.maximum(wanted - 1, 0)], (((0,), (0,)), ((), ())),
                preferred_element_type=jnp.float32,
            ).astype(send_ref.dtype)

    exchange_in_kernel(
        produce,
        lambda way, group, t: recv_ref.at[group * 8 + t if way == 0 else (t // 2 * 4 + group) * 2 + lax.rem(t, 2), way],
        send_ref, transit_ref, *sems,
    )
    wait_sends(coef_hops, coef_last)
    for copies in shared.values():
        for copy in copies:
            copy.wait_send()


def couple_kernel(
    slot_ref, pair_ref, side_ref, partner_ref, occ_ref, count_ref, fock_ref, energy_in_ref, rows_ref,
    recv_ref, energy_ref,
    part_ref, inbox_ref, weights_ref, sum_send, sum_recv, weight_send, weight_recv, energy_send, energy_recv,
    send_ref, transit_ref, *sems,
):
    share, width = part_ref.shape[1], part_ref.shape[2]
    pairs = count_ref.shape[0]
    mine = lax.axis_index("aux")
    greet()

    def part(d):
        first = lax.rem(mine + d, 4) * share

        @pl.loop(0, share)
        def _(t):
            k = jnp.minimum(first + t, pairs - 1)
            part_ref[d, t] = lax.dot_general(
                rows_ref[slot_ref[2 * k]],
                rows_ref[slot_ref[2 * k + 1]],
                (((1,), (1,)), ((), ())),
                preferred_element_type=jnp.float32,
            )

    sums = []
    for d in (2, 1, 3):
        part(d)
        sums.append(
            pltpu.make_async_remote_copy(
                src_ref=part_ref.at[d],
                dst_ref=inbox_ref.at[d - 1],
                send_sem=sum_send.at[d - 1],
                recv_sem=sum_recv.at[d - 1],
                device_id=plane(d),
                device_id_type=MESH,
            )
        )
        sums[-1].start()
    part(0)
    for copy in sums:
        copy.wait()

    row_id = lax.broadcasted_iota(jnp.int32, (width, width), 0)
    col_id = lax.broadcasted_iota(jnp.int32, (width, width), 1)

    @pl.loop(0, share)
    def _(t):
        k = jnp.minimum(mine * share + t, pairs - 1)
        coupling = (part_ref[0, t] + inbox_ref[0, t]) + (inbox_ref[1, t] + inbox_ref[2, t])
        by_col = jnp.broadcast_to(energy_in_ref[pl.ds(k, 1), :], (width, width))
        denom = by_col.T + by_col - fock_ref[occ_ref[2 * k]] - fock_ref[occ_ref[2 * k + 1]]
        inside = (row_id < count_ref[k]) & (col_id < count_ref[k])
        amplitude = jnp.where(inside, -coupling / denom, 0.0)
        mixed = 2.0 * amplitude - amplitude.T
        energy_ref[mine, pl.ds(t, 1), :] = jnp.sum(coupling * mixed, axis=0, keepdims=True)
        weights_ref[mine, t] = mixed.astype(jnp.bfloat16)

    copies = []
    for d in (2, 1, 3):
        for ref, out, got in ((weights_ref, weight_send, weight_recv), (energy_ref, energy_send, energy_recv)):
            copies.append(
                pltpu.make_async_remote_copy(
                    src_ref=ref.at[mine],
                    dst_ref=ref.at[mine],
                    send_sem=out.at[d - 1],
                    recv_sem=got.at[d - 1],
                    device_id=plane(d),
                    device_id_type=MESH,
                )
            )
            copies[-1].start()
    for copy in copies:
        copy.wait()

    def produce(way, d, group):
        @pl.loop(0, 8)
        def _(t):
            slot = slot_at(way, group, t)
            pair = pair_ref[slot]
            weights = weights_ref[pair // share, lax.rem(pair, share)].astype(jnp.float32)
            weights = jnp.where(side_ref[slot] == 0, weights, weights.T).astype(jnp.bfloat16)
            send_ref[way, group, t] = jnp.dot(
                weights, rows_ref[partner_ref[slot]], preferred_element_type=jnp.float32
            ).astype(send_ref.dtype)

    exchange_in_kernel(
        produce, lambda way, group, t: recv_ref.at[way, group, t], send_ref, transit_ref, *sems
    )


def grad_kernel(wanted_ref, coef_ref, gamma_ref, out_ref):
    step = pl.program_id(0)

    @pl.when(step == 0)
    def _():
        out_ref[...] = jnp.zeros_like(out_ref)

    for t in range(8):
        wanted = wanted_ref[slot_at_step(step, t)]

        @pl.when(wanted > 0)
        def _(t=t, wanted=wanted):
            coef = coef_ref[:, 0, 0, t].reshape(-1, coef_ref.shape[-1])
            term = jnp.dot(coef, gamma_ref[0, 0, t], preferred_element_type=jnp.float32).astype(jnp.bfloat16)
            out_ref[wanted - 1] += term.astype(jnp.float32)


def slot_at_step(step, t):
    group = lax.rem(step, 4)
    return jnp.where(step < 4, slot_at(0, group, t), slot_at(1, group, t))


def params(collective_id=None):
    return pltpu.CompilerParams(
        vmem_limit_bytes=VMEM_LIMIT, collective_id=collective_id, has_side_effects=collective_id is not None
    )


def local(three_index, fock_diag, pair_occ, pno_count, pno_energy, pno_coef):
    groups = lax.axis_size("pair")
    planes = lax.axis_size("aux")
    occ_dev, width_dom, width_aux = three_index.shape
    pair_dev = pair_occ.shape[0]
    width_pno = pno_coef.shape[3]
    halves = 2 * pair_dev
    slots = groups * CAPACITY
    part = width_dom // planes
    smem = pl.BlockSpec(memory_space=pltpu.SMEM)
    vmem = pl.BlockSpec(memory_space=pltpu.VMEM)
    hbm = pl.BlockSpec(memory_space=pl.ANY)

    slot_of, half_of, request, partner = plan_slots(pair_occ, groups, occ_dev)

    half = jnp.maximum(half_of, 0)
    coef_block = (part, width_pno)
    rows, coef, wanted = pl.pallas_call(
        fetch_kernel,
        name="fetch_coef_and_return_rows",
        out_shape=(
            jax.ShapeDtypeStruct((groups, CAPACITY, width_pno, width_aux), jnp.bfloat16),
            jax.ShapeDtypeStruct((planes, CAPACITY, 4, 8, part, width_pno), jnp.bfloat16),
            jax.ShapeDtypeStruct((slots,), jnp.int32),
        ),
        in_specs=[smem, vmem, vmem, hbm],
        out_specs=(hbm, vmem, smem),
        scratch_shapes=[
            pltpu.VMEM((occ_dev, width_dom, width_aux), jnp.bfloat16),
            pltpu.SemaphoreType.DMA,
            pltpu.VMEM((8, 4, 8, 128), jnp.int32),
            pltpu.SMEM((8, 4, 8, 128), jnp.int32),
            pltpu.SemaphoreType.DMA,
            pltpu.SemaphoreType.DMA((3,)),
            pltpu.SemaphoreType.DMA((3,)),
            pltpu.SemaphoreType.DMA((8,)),
            pltpu.SemaphoreType.DMA((8,)),
        ]
        + exchange_scratch(coef_block)
        + [pltpu.SemaphoreType.DMA((24,)), pltpu.SemaphoreType.DMA((24,))]
        + exchange_scratch((width_pno, width_aux)),
        compiler_params=params(1),
    )(
        half,
        jnp.pad(request[None, :], ((0, 7), (0, 128 - slots))),
        pno_coef.reshape(halves, width_dom, width_pno),
        three_index,
    )
    rows = rows.reshape(slots, width_pno, width_aux)

    share = -(-pair_dev // planes)
    gamma, energy_cols = pl.pallas_call(
        couple_kernel,
        name="couple_and_return_gamma",
        out_shape=(
            jax.ShapeDtypeStruct((CAPACITY, 4, 8, width_pno, width_aux), jnp.bfloat16),
            jax.ShapeDtypeStruct((planes, share, width_pno), jnp.float32),
        ),
        in_specs=[smem] * 7 + [vmem] * 2,
        out_specs=(hbm, vmem),
        scratch_shapes=[
            pltpu.VMEM((planes, share, width_pno, width_pno), jnp.float32),
            pltpu.VMEM((planes - 1, share, width_pno, width_pno), jnp.float32),
            pltpu.VMEM((planes, share, width_pno, width_pno), jnp.bfloat16),
        ]
        + [pltpu.SemaphoreType.DMA((planes - 1,))] * 6
        + exchange_scratch((width_pno, width_aux)),
        compiler_params=params(2),
    )(slot_of, half // 2, half % 2, partner, pair_occ.reshape(halves), pno_count, fock_diag, pno_energy, rows)
    energy = jnp.sum(energy_cols, axis=2).reshape(-1)[:pair_dev] / (width_pno * width_pno)
    grad = pl.pallas_call(
        grad_kernel,
        name="add_terms",
        out_shape=jax.ShapeDtypeStruct((occ_dev, width_dom, width_aux), jnp.float32),
        grid_spec=pltpu.PrefetchScalarGridSpec(
            num_scalar_prefetch=1,
            grid=(8,),
            in_specs=[
                pl.BlockSpec((planes, 1, 1, 8, part, width_pno), lambda s, w: (0, s // 4, s % 4, 0, 0, 0)),
                pl.BlockSpec((1, 1, 8, width_pno, width_aux), lambda s, w: (s // 4, s % 4, 0, 0, 0)),
            ],
            out_specs=pl.BlockSpec((occ_dev, width_dom, width_aux), lambda s, w: (0, 0, 0)),
        ),
        compiler_params=params(),
    )(wanted, coef, gamma)
    return energy, grad


def solution(mesh):
    placed = (
        P("pair", None, "aux"),
        P(),
        P("pair", None),
        P("pair"),
        P("pair", None),
        P("pair", None, None, None),
    )
    return jax.shard_map(
        local,
        mesh=mesh,
        in_specs=placed,
        out_specs=(P("pair"), P("pair", None, "aux")),
        check_vma=False,
    )
```

time: 425 us -> 323 us (0.76); the launches traced: 425 us -> 318 us
  waiting for transfers between devices: 198 us -> 0 us
  Pallas kernels: 158 us -> 311 us
  blocking collectives: 36.4 us -> 0 us
  between operations: 14.2 us -> 0.76 us
  starting transfers between devices: 7.48 us -> 0 us
    pallas_call x4 -> x2, Pallas kernels: 137 us -> 291 us  [the longest x1 151 us: local(): pl.pallas_call(couple_kernel, name='couple_and_return_gamma', out_shape=(...]
    all_to_all x1 -> x0, waiting for transfers between devices: 105 us -> none  [exchange(): lax.all_to_all(y, 'pair', split_axis=0, concat_axis=0, tiled=True)]
    psum x1 -> x0, waiting for transfers between devices: 58.6 us -> none  [local(): coupling = lax.psum(partial_sum, 'aux')]
    all_to_all x2 -> x0, blocking collectives: 36.4 us -> none  [exchange(): lax.all_to_all(y, 'pair', split_axis=0, concat_axis=0, tiled=True)]
    all_gather x1 -> x0, waiting for transfers between devices: 33.9 us -> none  [local(): coef = lax.all_gather(exchange(coef_part), 'aux')]
    all_to_all x1 -> x0, starting transfers between devices: 7.4 us -> none  [exchange(): lax.all_to_all(y, 'pair', split_axis=0, concat_axis=0, tiled=True)]
    unnamed x15 -> x11, local copies, waits for them, and re-layouts: 8.88 us -> 5.13 us
  transfers between devices with their start and end apart: 3 -> 0, of which waited for: 3 -> 0; matrix products, arithmetic and copies ran while one was open for 0% -> 0% of each run, Pallas kernels for 0% -> 0%
where the time goes in v3:
time: 323 us; the launch traced here: 318 us
  Pallas kernels  311 us (96%)
  local copies, waits for them, and re-layouts  5.6 us (2%)
    pallas_call x1, Pallas kernels, local(): pl.pallas_call(couple_kernel, name='couple_and_return_gamma', out_shape=(...  151 us
    pallas_call x1, Pallas kernels, local(): pl.pallas_call(fetch_kernel, name='fetch_coef_and_return_rows', out_shape...  140 us
    pallas_call x1, Pallas kernels, local(): pl.pallas_call(grad_kernel, name='add_terms', out_shape=jax.ShapeDtypeStr...  19.6 us

profile of v3, /device:TPU:0, one launch (start us, length us, event | category | flops | bytes accessed | tf_op | source)
XLA Modules:
  0.0 318.2 jit_solution(6248130138281373192)
XLA Ops:
  0.6 0.0 copy-start.2
  0.6 0.0 copy-start.4
  0.7 0.0 copy-start.3
  0.7 0.8 copy.18
  1.4 0.1 reshape.115.occ_ref
  1.6 0.2 convert_reduce_fusion
  1.8 0.1 reduce_sum.49
  1.9 0.1 rev.3
  2.0 0.1 mul.47
  2.1 0.2 select_reduce_fusion
  2.3 0.0 copy-start.1
  2.3 2.1 copy-done.1
  4.4 139.8 %fetch_coef_and_return_rows.1 = (bf16[32,2,128,512]{3,2,1,0:T(8,128)(2,1)}, bf16[4,2,4,8,64,128]{5,4,3,2,1,0:T(8,128)(2,1)}, s32[64]{0:T(128)S(1)}) custom-call(s32[64]{0:T(128)S(1)} %get-tuple-element.15.half_ref, s32[8,128]{1,0:T(8,128)S(1)} %pad.4.request_ref, bf16[62,256,128]{2,1,0:T(8,128)(2,1)S(1)} %bitcast.3, bf16[16,256,512]{2,1,0:T(8,128)(2,1)} %ints_hbm_ref.1), custom_call_target="tpu_custom_call" | custom-call | tf_op jit(solution)/shard_map/fetch_coef_and_return_rows/pallas_call | solution.py:406
  144.2 0.0 copy-done.2
  144.2 0.0 copy-done.4
  144.3 0.0 copy-done.3
  144.3 151.4 %couple_and_return_gamma.1 = (bf16[2,4,8,128,512]{4,3,2,1,0:T(8,128)(2,1)}, f32[4,8,128]{2,1,0:T(8,128)S(1)}) custom-call(s32[62]{0:T(128)S(1)} %multiply_add_fusion.slot_ref, s32[64]{0:T(128)S(1)} %get-tuple-element.17.pair_ref, s32[64]{0:T(128)S(1)} %get-tuple-element.16.side_ref, s32[64]{0:T(128)S(1)} %get-tuple-element.13.partner_ref, ...), custom_call_target="tpu_custom_call" | custom-call | tf_op jit(solution)/shard_map/couple_and_return_gamma/pallas_call | solution.py:440
  295.7 0.1 reduce_sum.52
  295.8 0.1 reshape.118
  295.9 0.5 slice_multiply_fusion
  296.4 0.0 copy-start
  296.4 2.2 copy-done
  298.6 19.6 %add_terms.1 = f32[16,256,512]{2,1,0:T(8,128)} custom-call(s32[64]{0:T(128)S(1)} %get-tuple-element.9.wanted_ref, bf16[4,2,4,8,64,128]{5,4,3,2,1,0:T(8,128)(2,1)S(1)} %copy-done, bf16[2,4,8,128,512]{4,3,2,1,0:T(8,128)(2,1)} %get-tuple-element.11.gamma_ref), custom_call_target="tpu_custom_call" | custom-call | tf_op jit(solution)/shard_map/add_terms/pallas_call | solution.py:459
  (5 shorter events, 0.1 us)
Async XLA Ops:
  0.6 143.6 %copy-start.2 = (f32[31,128]{1,0:T(8,128)S(1)}, f32[31,128]{1,0:T(8,128)}, u32[]{:S(2)}) copy-start(f32[31,128]{1,0:T(8,128)} %energy_in_ref.1) | copy-start | bytes 47620
  0.6 143.6 %copy-start.4 = (s32[31]{0:T(128)S(1)}, s32[31]{0:T(128)}, u32[]{:S(2)}) copy-start(s32[31]{0:T(128)} %count_ref.1) | copy-start | bytes 376
  0.7 143.6 %copy-start.3 = (f32[512]{0:T(512)S(1)}, f32[512]{0:T(512)}, u32[]{:S(2)}) copy-start(f32[512]{0:T(512)} %fock_ref.1) | copy-start | bytes 6148
  2.3 2.2 copy-start.1
  296.4 2.2 copy-start

commit v4 on v3

v4 whole, which is shorter than its diff:
```python
import functools

import jax
import jax.numpy as jnp
from jax import lax
from jax.experimental import pallas as pl
from jax.experimental.pallas import tpu as pltpu
from jax.sharding import PartitionSpec as P

CAPACITY = 2
MESH = pl.DeviceIdType.MESH
GROUP_ORDER = (1, 3, 2, 0)
OWN_FIRST = (0, 1, 3, 2)
SUMMED_IN_PARTS = 2


def plan_slots(pair_occ, groups, occ_dev):
    occ_flat = pair_occ.reshape(-1)
    halves = occ_flat.shape[0]
    owner = occ_flat // occ_dev
    half_ids = jnp.arange(halves, dtype=jnp.int32)
    earlier = (owner[None, :] == owner[:, None]) & (half_ids[None, :] < half_ids[:, None])
    rank = jnp.sum(earlier.astype(jnp.int32), axis=1)
    slot_of = owner * CAPACITY + rank
    hot = (slot_of[None, :] == jnp.arange(groups * CAPACITY, dtype=jnp.int32)[:, None]).astype(jnp.int32)
    half_of = jnp.sum(hot * (half_ids + 1)[None, :], axis=1) - 1
    request = jnp.sum(hot * (occ_flat % occ_dev + 1)[None, :], axis=1)
    partner = jnp.sum(hot * slot_of.reshape(-1, 2)[:, ::-1].reshape(-1)[None, :], axis=1)
    return slot_of, half_of, request, partner


def place():
    me = lax.axis_index("pair")
    return me // 8, lax.rem(me // 2, 4), lax.rem(me, 2)


def device(z, y, core):
    return {"pair": (z * 4 + y) * 2 + core}


def plane(d):
    return {"aux": lax.rem(lax.axis_index("aux") + d, 4)}


def greet():
    z, y, core = place()
    barrier = pltpu.get_barrier_semaphore()
    peers = [device(z, y, 1 - core)]
    for d in (1, 2, 3):
        peers.append(plane(d))
        for c in (core, 1 - core):
            peers += [device(lax.rem(z + d, 4), y, c), device(z, lax.rem(y + d, 4), c)]
    for peer in peers:
        pl.semaphore_signal(barrier, inc=1, device_id=peer, device_id_type=MESH)
    pl.semaphore_wait(barrier, len(peers))


def start_exchange(produce, deliver, order, between, send, transit, hop_send, hop_recv, last_send, last_recv):
    z, y, core = place()
    here, across = (z, y), (y, z)
    hops, last = {}, {}

    def hop(way, d):
        group, n = lax.rem(here[way] + d, 4), way * 3 + d - 1
        hops[way, d] = pltpu.make_async_remote_copy(
            src_ref=send.at[way, group],
            dst_ref=transit.at[way, here[way]],
            send_sem=hop_send.at[n],
            recv_sem=hop_recv.at[n],
            device_id=device(group, y, core) if way == 0 else device(z, group, core),
            device_id_type=MESH,
        )
        hops[way, d].start()

    def spread(way, ds):
        source = lax.rem(here[way] + 4 - ds, 4)
        last[way, ds] = []
        for d in GROUP_ORDER:
            for dc in (0, 1):
                to, to_core = lax.rem(across[way] + d, 4), lax.rem(core + dc, 2)
                block = (transit if ds else send).at[way, source, to * 2 + to_core]
                dst = deliver(way, source, across[way] * 2 + core)
                n = ((way * 4 + ds) * 4 + d) * 2 + dc
                if d == 0 and dc == 0:
                    copy = pltpu.make_async_copy(block, dst, last_send.at[n])
                else:
                    copy = pltpu.make_async_remote_copy(
                        src_ref=block,
                        dst_ref=dst,
                        send_sem=last_send.at[n],
                        recv_sem=last_recv.at[n],
                        device_id=device(z, to, to_core) if way == 0 else device(to, y, to_core),
                        device_id_type=MESH,
                    )
                copy.start()
                last[way, ds].append((copy, d > 0 or dc > 0))

    for d in order:
        for way in (0, 1):
            produce(way, d, lax.rem(here[way] + d, 4))
            if d:
                hop(way, d)
            else:
                spread(way, 0)
    between()
    for ds in (1, 3, 2):
        for way in (0, 1):
            hops[way, ds].wait_recv()
            spread(way, ds)
    return hops, last


def wait_arrivals(copies):
    for copy, remote in copies:
        if remote:
            copy.wait_recv()
        else:
            copy.wait()


def wait_sends(hops, last):
    for hop in hops.values():
        hop.wait_send()
    for copies in last.values():
        for copy, remote in copies:
            if remote:
                copy.wait_send()


def exchange_in_kernel(produce, deliver, order, *scratch):
    hops, last = start_exchange(produce, deliver, order, lambda: None, *scratch)
    for copies in last.values():
        wait_arrivals(copies)
    wait_sends(hops, last)


def exchange_scratch(shape):
    return [
        pltpu.VMEM((2, 4, 8) + shape, jnp.bfloat16),
        pltpu.VMEM((2, 4, 8) + shape, jnp.bfloat16),
        pltpu.SemaphoreType.DMA((6,)),
        pltpu.SemaphoreType.DMA((6,)),
        pltpu.SemaphoreType.DMA((64,)),
        pltpu.SemaphoreType.DMA((64,)),
    ]


def slot_at(way, group, t):
    owner = group * 8 + t if way == 0 else (t // 2 * 4 + group) * 2 + lax.rem(t, 2)
    return owner * CAPACITY + way


def table_hops(table, send, recv):
    z, y, core = place()
    mine = y * 2 + core
    copies = []
    for d in (1, 3, 2):
        copies.append(
            pltpu.make_async_remote_copy(
                src_ref=table.at[mine, z],
                dst_ref=table.at[mine, z],
                send_sem=send.at[d - 1],
                recv_sem=recv.at[d - 1],
                device_id=device(lax.rem(z + d, 4), y, core),
                device_id_type=MESH,
            )
        )
        copies[-1].start()
    return copies


def table_spread(table, send, recv):
    z, y, core = place()
    mine = y * 2 + core
    copies = []
    for d in GROUP_ORDER:
        for dc in (0, 1):
            if d or dc:
                n = d * 2 + dc
                copies.append(
                    pltpu.make_async_remote_copy(
                        src_ref=table.at[mine],
                        dst_ref=table.at[mine],
                        send_sem=send.at[n],
                        recv_sem=recv.at[n],
                        device_id=device(z, lax.rem(y + d, 4), lax.rem(core + dc, 2)),
                        device_id_type=MESH,
                    )
                )
                copies[-1].start()
    return copies


def fetch_kernel(
    half_ref, request_ref, coef_hbm_ref, ints_hbm_ref,
    recv_ref, coef_ref, wanted_ref,
    own_coef_ref, own_coef_sem, ints_ref, ints_sem, table_ref, table_smem, table_sem,
    table_hop_send, table_hop_recv, table_last_send, table_last_recv,
    coef_send_ref, coef_transit_ref, coef_hop_send, coef_hop_recv, coef_last_send, coef_last_recv,
    plane_send, plane_recv,
    send_ref, transit_ref, *sems,
):
    z, y, core = place()
    here = (z, y)
    mine = lax.axis_index("aux")
    rows = coef_ref.shape[4]
    first = pl.multiple_of(mine * rows, rows)
    load_coef = pltpu.make_async_copy(coef_hbm_ref.at[:, pl.ds(first, rows)], own_coef_ref, own_coef_sem)
    load_coef.start()
    load = pltpu.make_async_copy(ints_hbm_ref, ints_ref, ints_sem)
    load.start()
    table_ref[y * 2 + core, z] = request_ref[...]
    greet()
    tables = table_hops(table_ref, table_hop_send, table_hop_recv)
    load_coef.wait()

    def pick(way, d, group):
        @pl.loop(0, 8)
        def _(t):
            coef_send_ref[way, group, t] = own_coef_ref[half_ref[slot_at(way, group, t)]]

    spread_tables = []

    def between():
        for copy in tables:
            copy.wait()
        spread_tables.extend(table_spread(table_ref, table_last_send, table_last_recv))

    coef_hops, coef_last = start_exchange(
        pick,
        lambda way, group, t: coef_ref.at[mine, way, group, t],
        OWN_FIRST,
        between,
        coef_send_ref, coef_transit_ref, coef_hop_send, coef_hop_recv, coef_last_send, coef_last_recv,
    )

    batches = [(way, (4 - d) % 4) for d in OWN_FIRST for way in (0, 1)]
    shared = {}

    def to_plane(way, ds, source, d, part, n):
        block = coef_ref.at[lax.rem(mine + source, 4), way, lax.rem(here[way] + 4 - ds, 4), part]
        n += (way * 4 + ds) * 4
        copy = pltpu.make_async_remote_copy(
            src_ref=block,
            dst_ref=block,
            send_sem=plane_send.at[n],
            recv_sem=plane_recv.at[n],
            device_id=plane(d),
            device_id_type=MESH,
        )
        copy.start()
        shared.setdefault((way, ds), []).append(copy)

    def share(way, ds):
        wait_arrivals(coef_last[way, ds])
        to_plane(way, ds, 0, 1, pl.ds(0, 8), 0)
        to_plane(way, ds, 0, 3, pl.ds(0, 8), 1)

    def pass_on(way, ds):
        shared[way, ds][0].wait_recv()
        to_plane(way, ds, 3, 1, pl.ds(0, 4), 2)
        shared[way, ds][1].wait_recv()
        to_plane(way, ds, 1, 3, pl.ds(4, 4), 3)

    share(*batches[0])
    share(*batches[1])
    pass_on(*batches[0])
    for copy in spread_tables:
        copy.wait()
    to_smem = pltpu.make_async_copy(table_ref, table_smem, table_sem)
    to_smem.start()
    to_smem.wait()
    load.wait()
    me = lax.axis_index("pair")

    def produce(way, d, group):
        n = batches.index((way, (4 - d) % 4))
        if n + 2 < len(batches):
            share(*batches[n + 2])
        if n + 1 < len(batches):
            pass_on(*batches[n + 1])
        for copy in shared[batches[n]][2:]:
            copy.wait_recv()

        @pl.loop(0, 8)
        def _(t):
            slot = slot_at(way, group, t)
            owner = slot // CAPACITY
            wanted = table_smem[lax.rem(owner, 8), owner // 8, 0, me * CAPACITY + way]
            wanted_ref[slot] = wanted
            coef = coef_ref[:, way, group, t].reshape(-1, coef_ref.shape[-1])
            send_ref[way, group, t] = lax.dot_general(
                coef, ints_ref[jnp.maximum(wanted - 1, 0)], (((0,), (0,)), ((), ())),
                preferred_element_type=jnp.float32,
            ).astype(send_ref.dtype)

    exchange_in_kernel(
        produce,
        lambda way, group, t: recv_ref.at[group * 8 + t if way == 0 else (t // 2 * 4 + group) * 2 + lax.rem(t, 2), way],
        OWN_FIRST,
        send_ref, transit_ref, *sems,
    )
    wait_sends(coef_hops, coef_last)
    for copies in shared.values():
        for copy in copies:
            copy.wait_send()


def couple_kernel(
    slot_ref, pair_ref, side_ref, partner_ref, occ_ref, count_ref, fock_ref, energy_in_ref, rows_ref,
    recv_ref, energy_ref,
    own_ref, part_ref, inbox_ref, weights_ref, sum_send, sum_recv, weight_send, weight_recv, energy_send, energy_recv,
    send_ref, transit_ref, *sems,
):
    share, width, _ = own_ref.shape
    pairs = count_ref.shape[0]
    mine = lax.axis_index("aux")
    greet()

    size = share // SUMMED_IN_PARTS

    def couplings(d, b, out_ref):
        first = lax.rem(mine + d, 4) * share + b * size

        @pl.loop(0, size)
        def _(t):
            k = jnp.minimum(first + t, pairs - 1)
            out_ref[b * size + t] = lax.dot_general(
                rows_ref[slot_ref[2 * k]],
                rows_ref[slot_ref[2 * k + 1]],
                (((1,), (1,)), ((), ())),
                preferred_element_type=jnp.float32,
            ).astype(out_ref.dtype)

    sums = {}
    for b in range(SUMMED_IN_PARTS):
        for d in (2, 1, 3):
            couplings(d, b, part_ref.at[d - 1])
            n = b * 3 + d - 1
            sums[b, d] = pltpu.make_async_remote_copy(
                src_ref=part_ref.at[d - 1, pl.ds(b * size, size)],
                dst_ref=inbox_ref.at[d - 1, pl.ds(b * size, size)],
                send_sem=sum_send.at[n],
                recv_sem=sum_recv.at[n],
                device_id=plane(d),
                device_id_type=MESH,
            )
            sums[b, d].start()
    for b in range(SUMMED_IN_PARTS):
        couplings(0, b, own_ref)

    row_id = lax.broadcasted_iota(jnp.int32, (width, width), 0)
    col_id = lax.broadcasted_iota(jnp.int32, (width, width), 1)

    def weigh(t):
        k = jnp.minimum(mine * share + t, pairs - 1)
        others = [inbox_ref[n, t].astype(jnp.float32) for n in range(3)]
        coupling = (own_ref[t] + others[0]) + (others[1] + others[2])
        by_col = jnp.broadcast_to(energy_in_ref[pl.ds(k, 1), :], (width, width))
        denom = by_col.T + by_col - fock_ref[occ_ref[2 * k]] - fock_ref[occ_ref[2 * k + 1]]
        inside = (row_id < count_ref[k]) & (col_id < count_ref[k])
        amplitude = jnp.where(inside, -coupling / denom, 0.0)
        mixed = 2.0 * amplitude - amplitude.T
        energy_ref[mine, pl.ds(t, 1), :] = jnp.sum(coupling * mixed, axis=0, keepdims=True)
        weights_ref[mine, t] = mixed.astype(jnp.bfloat16)

    copies = []

    def tell(ref, send, recv, n, d):
        copies.append(
            pltpu.make_async_remote_copy(
                src_ref=ref,
                dst_ref=ref,
                send_sem=send.at[n],
                recv_sem=recv.at[n],
                device_id=plane(d),
                device_id_type=MESH,
            )
        )
        copies[-1].start()

    for b in range(SUMMED_IN_PARTS):
        for d in (2, 1, 3):
            sums[b, d].wait_recv()
        pl.loop(b * size, (b + 1) * size)(weigh)
        for d in (2, 1, 3):
            tell(weights_ref.at[mine, pl.ds(b * size, size)], weight_send, weight_recv, b * 3 + d - 1, d)
    for d in (2, 1, 3):
        tell(energy_ref.at[mine], energy_send, energy_recv, d - 1, d)
    for copy in copies:
        copy.wait()
    for copy in sums.values():
        copy.wait_send()

    def produce(way, d, group):
        @pl.loop(0, 8)
        def _(t):
            slot = slot_at(way, group, t)
            pair = pair_ref[slot]
            weights = weights_ref[pair // share, lax.rem(pair, share)].astype(jnp.float32)
            weights = jnp.where(side_ref[slot] == 0, weights, weights.T).astype(jnp.bfloat16)
            send_ref[way, group, t] = jnp.dot(
                weights, rows_ref[partner_ref[slot]], preferred_element_type=jnp.float32
            ).astype(send_ref.dtype)

    exchange_in_kernel(
        produce, lambda way, group, t: recv_ref.at[way, group, t], OWN_FIRST, send_ref, transit_ref, *sems
    )


def grad_kernel(wanted_ref, coef_ref, gamma_ref, out_ref):
    step = pl.program_id(0)

    @pl.when(step == 0)
    def _():
        out_ref[...] = jnp.zeros_like(out_ref)

    for t in range(8):
        wanted = wanted_ref[slot_at_step(step, t)]
        coef = coef_ref[:, 0, 0, t].reshape(-1, coef_ref.shape[-1])
        coef = jnp.where(wanted > 0, coef, jnp.zeros_like(coef))
        term = jnp.dot(coef, gamma_ref[0, 0, t], preferred_element_type=jnp.float32).astype(jnp.bfloat16)
        out_ref[jnp.maximum(wanted - 1, 0)] += term.astype(jnp.float32)


def slot_at_step(step, t):
    group = lax.rem(step, 4)
    return jnp.where(step < 4, slot_at(0, group, t), slot_at(1, group, t))


def params(limit, collective_id=None):
    return pltpu.CompilerParams(
        vmem_limit_bytes=limit << 20, collective_id=collective_id, has_side_effects=collective_id is not None
    )


def local(three_index, fock_diag, pair_occ, pno_count, pno_energy, pno_coef):
    groups = lax.axis_size("pair")
    planes = lax.axis_size("aux")
    occ_dev, width_dom, width_aux = three_index.shape
    pair_dev = pair_occ.shape[0]
    width_pno = pno_coef.shape[3]
    halves = 2 * pair_dev
    slots = groups * CAPACITY
    part = width_dom // planes
    smem = pl.BlockSpec(memory_space=pltpu.SMEM)
    vmem = pl.BlockSpec(memory_space=pltpu.VMEM)
    hbm = pl.BlockSpec(memory_space=pl.ANY)

    slot_of, half_of, request, partner = plan_slots(pair_occ, groups, occ_dev)

    half = jnp.maximum(half_of, 0)
    coef_block = (part, width_pno)
    rows, coef, wanted = pl.pallas_call(
        fetch_kernel,
        name="fetch_coef_and_return_rows",
        out_shape=(
            pltpu.VMEM((groups, CAPACITY, width_pno, width_aux), jnp.bfloat16),
            jax.ShapeDtypeStruct((planes, CAPACITY, 4, 8, part, width_pno), jnp.bfloat16),
            jax.ShapeDtypeStruct((slots,), jnp.int32),
        ),
        in_specs=[smem, vmem, hbm, hbm],
        out_specs=(vmem, vmem, smem),
        scratch_shapes=[
            pltpu.VMEM((halves, part, width_pno), jnp.bfloat16),
            pltpu.SemaphoreType.DMA,
            pltpu.VMEM((occ_dev, width_dom, width_aux), jnp.bfloat16),
            pltpu.SemaphoreType.DMA,
            pltpu.VMEM((8, 4, 8, 128), jnp.int32),
            pltpu.SMEM((8, 4, 8, 128), jnp.int32),
            pltpu.SemaphoreType.DMA,
            pltpu.SemaphoreType.DMA((3,)),
            pltpu.SemaphoreType.DMA((3,)),
            pltpu.SemaphoreType.DMA((8,)),
            pltpu.SemaphoreType.DMA((8,)),
        ]
        + exchange_scratch(coef_block)
        + [pltpu.SemaphoreType.DMA((32,)), pltpu.SemaphoreType.DMA((32,))]
        + exchange_scratch((width_pno, width_aux)),
        compiler_params=params(49, 1),
    )(
        half,
        jnp.pad(request[None, :], ((0, 7), (0, 128 - slots))),
        pltpu.with_memory_space_constraint(pno_coef.reshape(halves, width_dom, width_pno), pltpu.HBM),
        pltpu.with_memory_space_constraint(three_index, pltpu.HBM),
    )
    rows = rows.reshape(slots, width_pno, width_aux)

    share = -(-pair_dev // planes)
    gamma, energy_cols = pl.pallas_call(
        couple_kernel,
        name="couple_and_return_gamma",
        out_shape=(
            jax.ShapeDtypeStruct((CAPACITY, 4, 8, width_pno, width_aux), jnp.bfloat16),
            jax.ShapeDtypeStruct((planes, share, width_pno), jnp.float32),
        ),
        in_specs=[smem] * 7 + [vmem] * 2,
        out_specs=(hbm, vmem),
        scratch_shapes=[
            pltpu.VMEM((share, width_pno, width_pno), jnp.float32),
            pltpu.VMEM((planes - 1, share, width_pno, width_pno), jnp.bfloat16),
            pltpu.VMEM((planes - 1, share, width_pno, width_pno), jnp.bfloat16),
            pltpu.VMEM((planes, share, width_pno, width_pno), jnp.bfloat16),
        ]
        + [pltpu.SemaphoreType.DMA((SUMMED_IN_PARTS * (planes - 1),))] * 4
        + [pltpu.SemaphoreType.DMA((planes - 1,))] * 2
        + exchange_scratch((width_pno, width_aux)),
        compiler_params=params(49, 2),
    )(slot_of, half // 2, half % 2, partner, pair_occ.reshape(halves), pno_count, fock_diag, pno_energy, rows)
    energy = jnp.sum(energy_cols, axis=2).reshape(-1)[:pair_dev] / (width_pno * width_pno)
    grad = pl.pallas_call(
        grad_kernel,
        name="add_terms",
        out_shape=jax.ShapeDtypeStruct((occ_dev, width_dom, width_aux), jnp.float32),
        grid_spec=pltpu.PrefetchScalarGridSpec(
            num_scalar_prefetch=1,
            grid=(8,),
            in_specs=[
                pl.BlockSpec((planes, 1, 1, 8, part, width_pno), lambda s, w: (0, s // 4, s % 4, 0, 0, 0)),
                pl.BlockSpec((1, 1, 8, width_pno, width_aux), lambda s, w: (s // 4, s % 4, 0, 0, 0)),
            ],
            out_specs=pl.BlockSpec((occ_dev, width_dom, width_aux), lambda s, w: (0, 0, 0)),
        ),
        compiler_params=params(49),
    )(wanted, *(pltpu.with_memory_space_constraint(x, pltpu.HBM) for x in (coef, gamma)))
    return energy, grad


def solution(mesh):
    placed = (
        P("pair", None, "aux"),
        P(),
        P("pair", None),
        P("pair"),
        P("pair", None),
        P("pair", None, None, None),
    )
    return jax.shard_map(
        local,
        mesh=mesh,
        in_specs=placed,
        out_specs=(P("pair"), P("pair", None, "aux")),
        check_vma=False,
    )
```

time: 323 us -> 286 us (0.89)
  Pallas kernels: 311 us -> 276 us
    pallas_call x1, Pallas kernels: 151 us -> 129 us  [local(): pl.pallas_call(couple_kernel, name='couple_and_return_gamma', out_shape=(...]
    pallas_call x1, Pallas kernels: 140 us -> 133 us  [local(): pl.pallas_call(fetch_kernel, name='fetch_coef_and_return_rows', out_shape...]
    pallas_call x1, Pallas kernels: 19.6 us -> 14 us  [local(): pl.pallas_call(grad_kernel, name='add_terms', out_shape=jax.ShapeDtypeStr...]
where the time goes in v4:
time: 286 us; the launch traced here: 284 us
  Pallas kernels  276 us (97%)
  local copies, waits for them, and re-layouts  5.25 us (2%)
    pallas_call x1, Pallas kernels, local(): pl.pallas_call(fetch_kernel, name='fetch_coef_and_return_rows', out_shape...  133 us
    pallas_call x1, Pallas kernels, local(): pl.pallas_call(couple_kernel, name='couple_and_return_gamma', out_shape=(...  129 us
    pallas_call x1, Pallas kernels, local(): pl.pallas_call(grad_kernel, name='add_terms', out_shape=jax.ShapeDtypeStr...  14 us

profile of v4, /device:TPU:0, one launch (start us, length us, event | category | flops | bytes accessed | tf_op | source)
XLA Modules:
  0.0 283.9 jit_solution(7365914161803332877)
XLA Ops:
  0.6 0.0 copy-start.1
  0.6 0.0 copy-start.3
  0.7 0.0 copy-start.2
  0.7 0.8 copy.18
  1.4 0.1 reshape.115.occ_ref
  1.6 0.2 convert_reduce_fusion
  1.8 0.1 reduce_sum.49
  1.9 0.1 rev.3
  2.0 0.1 mul.47
  2.1 0.2 select_reduce_fusion
  2.2 0.5 add_maximum_fusion
  2.7 0.6 pad.4.request_ref
  3.3 133.2 %fetch_coef_and_return_rows.1 = (bf16[32,2,128,512]{3,2,1,0:T(8,128)(2,1)S(1)}, bf16[4,2,4,8,64,128]{5,4,3,2,1,0:T(8,128)(2,1)}, s32[64]{0:T(128)}) custom-call(s32[64]{0:T(128)} %get-tuple-element.15.half_ref, s32[8,128]{1,0:T(8,128)} %pad.4.request_ref, bf16[62,256,128]{2,1,0:T(8,128)(2,1)} %bitcast.4, bf16[16,256,512]{2,1,0:T(8,128)(2,1)} %ints_hbm_ref.1), custom_call_target="tpu_custom_call" | custom-call | tf_op jit(solution)/shard_map/fetch_coef_and_return_rows/pallas_call | solution.py:454
  136.5 0.0 copy-start
  136.5 3.4 %copy-done = bf16[32,2,128,512]{3,2,1,0:T(8,128)(2,1)} copy-done((bf16[32,2,128,512]{3,2,1,0:T(8,128)(2,1)}, bf16[32,2,128,512]{3,2,1,0:T(8,128)(2,1)S(1)}, u32[]{:S(2)}) %copy-start) | copy-done | bytes 8388632
  139.9 0.0 copy-start.4
  139.9 0.0 copy-done.1
  139.9 0.0 copy-done.3
  139.9 0.0 copy-done.2
  139.9 129.3 %couple_and_return_gamma.1 = (bf16[2,4,8,128,512]{4,3,2,1,0:T(8,128)(2,1)}, f32[4,8,128]{2,1,0:T(8,128)S(1)}) custom-call(s32[62]{0:T(128)S(1)} %multiply_add_fusion.slot_ref, s32[64]{0:T(128)S(1)} %get-tuple-element.17.pair_ref, s32[64]{0:T(128)S(1)} %get-tuple-element.16.side_ref, s32[64]{0:T(128)S(1)} %get-tuple-element.13.partner_ref, ...), custom_call_target="tpu_custom_call" | custom-call | tf_op jit(solution)/shard_map/couple_and_return_gamma/pallas_call | solution.py:490
  269.3 0.1 reduce_sum.52
  269.4 0.1 reshape.118
  269.4 0.5 slice_multiply_fusion
  270.0 0.0 copy-done.4
  270.0 14.0 %add_terms.1 = f32[16,256,512]{2,1,0:T(8,128)} custom-call(s32[64]{0:T(128)S(1)} %copy-done.4, bf16[4,2,4,8,64,128]{5,4,3,2,1,0:T(8,128)(2,1)} %get-tuple-element.10.coef_ref, bf16[2,4,8,128,512]{4,3,2,1,0:T(8,128)(2,1)} %get-tuple-element.11.gamma_ref), custom_call_target="tpu_custom_call" | custom-call | tf_op jit(solution)/shard_map/add_terms/pallas_call | solution.py:511
  (3 shorter events, 0.0 us)
Async XLA Ops:
  0.6 139.3 %copy-start.1 = (f32[31,128]{1,0:T(8,128)S(1)}, f32[31,128]{1,0:T(8,128)}, u32[]{:S(2)}) copy-start(f32[31,128]{1,0:T(8,128)} %energy_in_ref.1) | copy-start | bytes 47620
  0.6 139.3 %copy-start.3 = (s32[31]{0:T(128)S(1)}, s32[31]{0:T(128)}, u32[]{:S(2)}) copy-start(s32[31]{0:T(128)} %count_ref.1) | copy-start | bytes 376
  0.7 139.3 %copy-start.2 = (f32[512]{0:T(512)S(1)}, f32[512]{0:T(512)}, u32[]{:S(2)}) copy-start(f32[512]{0:T(512)} %fock_ref.1) | copy-start | bytes 6148
  136.5 3.4 %copy-start = (bf16[32,2,128,512]{3,2,1,0:T(8,128)(2,1)}, bf16[32,2,128,512]{3,2,1,0:T(8,128)(2,1)S(1)}, u32[]{:S(2)}) copy-start(bf16[32,2,128,512]{3,2,1,0:T(8,128)(2,1)S(1)} %get-tuple-element.7) | copy-start | bytes 25165828
  139.9 130.1 %copy-start.4 = (s32[64]{0:T(128)S(1)}, s32[64]{0:T(128)}, u32[]{:S(2)}) copy-start(s32[64]{0:T(128)} %get-tuple-element.9.wanted_ref) | copy-start | bytes 772

commit v5 on v4

--- a/solution.py
+++ b/solution.py
@@ -55,10 +55,10 @@
     pl.semaphore_wait(barrier, len(peers))
 
 
-def start_exchange(produce, deliver, order, between, send, transit, hop_send, hop_recv, last_send, last_recv):
+def start_exchange(produce, deliver, order, between, last, send, transit, hop_send, hop_recv, last_send, last_recv):
     z, y, core = place()
     here, across = (z, y), (y, z)
-    hops, last = {}, {}
+    hops = {}
 
     def hop(way, d):
         group, n = lax.rem(here[way] + d, 4), way * 3 + d - 1
@@ -128,7 +128,7 @@
 
 
 def exchange_in_kernel(produce, deliver, order, *scratch):
-    hops, last = start_exchange(produce, deliver, order, lambda: None, *scratch)
+    hops, last = start_exchange(produce, deliver, order, lambda: None, {}, *scratch)
     for copies in last.values():
         wait_arrivals(copies)
     wait_sends(hops, last)
@@ -191,15 +191,16 @@
     return copies
 
 
-def fetch_kernel(
+def fetch_rows(
     half_ref, request_ref, coef_hbm_ref, ints_hbm_ref,
-    recv_ref, coef_ref, wanted_ref,
+    rows_ref, coef_ref, wanted_ref,
     own_coef_ref, own_coef_sem, ints_ref, ints_sem, table_ref, table_smem, table_sem,
     table_hop_send, table_hop_recv, table_last_send, table_last_recv,
     coef_send_ref, coef_transit_ref, coef_hop_send, coef_hop_recv, coef_last_send, coef_last_recv,
     plane_send, plane_recv,
-    send_ref, transit_ref, *sems,
+    *exchange,
 ):
+    send_ref = exchange[0]
     z, y, core = place()
     here = (z, y)
     mine = lax.axis_index("aux")
@@ -220,20 +221,7 @@
             coef_send_ref[way, group, t] = own_coef_ref[half_ref[slot_at(way, group, t)]]
 
     spread_tables = []
-
-    def between():
-        for copy in tables:
-            copy.wait()
-        spread_tables.extend(table_spread(table_ref, table_last_send, table_last_recv))
-
-    coef_hops, coef_last = start_exchange(
-        pick,
-        lambda way, group, t: coef_ref.at[mine, way, group, t],
-        OWN_FIRST,
-        between,
-        coef_send_ref, coef_transit_ref, coef_hop_send, coef_hop_recv, coef_last_send, coef_last_recv,
-    )
-
+    coef_last = {}
     batches = [(way, (4 - d) % 4) for d in OWN_FIRST for way in (0, 1)]
     shared = {}
 
@@ -262,8 +250,22 @@
         shared[way, ds][1].wait_recv()
         to_plane(way, ds, 1, 3, pl.ds(4, 4), 3)
 
-    share(*batches[0])
-    share(*batches[1])
+    def between():
+        for copy in tables:
+            copy.wait()
+        spread_tables.extend(table_spread(table_ref, table_last_send, table_last_recv))
+        share(*batches[0])
+        share(*batches[1])
+
+    coef_hops, _ = start_exchange(
+        pick,
+        lambda way, group, t: coef_ref.at[mine, way, group, t],
+        OWN_FIRST,
+        between,
+        coef_last,
+        coef_send_ref, coef_transit_ref, coef_hop_send, coef_hop_recv, coef_last_send, coef_last_recv,
+    )
+
     pass_on(*batches[0])
     for copy in spread_tables:
         copy.wait()
@@ -296,9 +298,9 @@
 
     exchange_in_kernel(
         produce,
-        lambda way, group, t: recv_ref.at[group * 8 + t if way == 0 else (t // 2 * 4 + group) * 2 + lax.rem(t, 2), way],
+        lambda way, group, t: rows_ref.at[slot_at(way, group, t)],
         OWN_FIRST,
-        send_ref, transit_ref, *sems,
+        *exchange,
     )
     wait_sends(coef_hops, coef_last)
     for copies in shared.values():
@@ -306,16 +308,16 @@
             copy.wait_send()
 
 
-def couple_kernel(
+def couple_and_weigh(
     slot_ref, pair_ref, side_ref, partner_ref, occ_ref, count_ref, fock_ref, energy_in_ref, rows_ref,
     recv_ref, energy_ref,
     own_ref, part_ref, inbox_ref, weights_ref, sum_send, sum_recv, weight_send, weight_recv, energy_send, energy_recv,
-    send_ref, transit_ref, *sems,
+    *exchange,
 ):
     share, width, _ = own_ref.shape
     pairs = count_ref.shape[0]
     mine = lax.axis_index("aux")
-    greet()
+    send_ref = exchange[0]
 
     size = share // SUMMED_IN_PARTS
 
@@ -404,7 +406,25 @@
             ).astype(send_ref.dtype)
 
     exchange_in_kernel(
-        produce, lambda way, group, t: recv_ref.at[way, group, t], OWN_FIRST, send_ref, transit_ref, *sems
+        produce, lambda way, group, t: recv_ref.at[way, group, t], OWN_FIRST, *exchange
+    )
+
+
+def pairs_kernel(
+    half_ref, slot_ref, pair_ref, side_ref, partner_ref, occ_ref, count_ref, fock_ref, request_ref, energy_in_ref,
+    coef_hbm_ref, ints_hbm_ref,
+    gamma_ref, coef_ref, wanted_ref, energy_ref,
+    rows_ref, *scratch,
+):
+    fetch, couple, (send_ref, transit_rows, transit_gamma), sems = scratch[:19], scratch[19:29], scratch[29:32], scratch[32:]
+    fetch_rows(
+        half_ref, request_ref, coef_hbm_ref, ints_hbm_ref, rows_ref, coef_ref, wanted_ref, *fetch,
+        send_ref, transit_rows, *sems[:4],
+    )
+    couple_and_weigh(
+        slot_ref, pair_ref, side_ref, partner_ref, occ_ref, count_ref, fock_ref, energy_in_ref, rows_ref,
+        gamma_ref, energy_ref, *couple,
+        send_ref, transit_gamma, *sems[4:],
     )
 
 
@@ -451,17 +471,21 @@
 
     half = jnp.maximum(half_of, 0)
     coef_block = (part, width_pno)
-    rows, coef, wanted = pl.pallas_call(
-        fetch_kernel,
-        name="fetch_coef_and_return_rows",
+    share = -(-pair_dev // planes)
+    row_block = exchange_scratch((width_pno, width_aux))
+    gamma, coef, wanted, energy_cols = pl.pallas_call(
+        pairs_kernel,
+        name="pairs",
         out_shape=(
-            pltpu.VMEM((groups, CAPACITY, width_pno, width_aux), jnp.bfloat16),
+            jax.ShapeDtypeStruct((CAPACITY, 4, 8, width_pno, width_aux), jnp.bfloat16),
             jax.ShapeDtypeStruct((planes, CAPACITY, 4, 8, part, width_pno), jnp.bfloat16),
             jax.ShapeDtypeStruct((slots,), jnp.int32),
+            jax.ShapeDtypeStruct((planes, share, width_pno), jnp.float32),
         ),
-        in_specs=[smem, vmem, hbm, hbm],
-        out_specs=(vmem, vmem, smem),
+        in_specs=[smem] * 8 + [vmem] * 2 + [hbm] * 2,
+        out_specs=(hbm, vmem, smem, vmem),
         scratch_shapes=[
+            pltpu.VMEM((slots, width_pno, width_aux), jnp.bfloat16),
             pltpu.VMEM((halves, part, width_pno), jnp.bfloat16),
             pltpu.SemaphoreType.DMA,
             pltpu.VMEM((occ_dev, width_dom, width_aux), jnp.bfloat16),
@@ -476,27 +500,7 @@
         ]
         + exchange_scratch(coef_block)
         + [pltpu.SemaphoreType.DMA((32,)), pltpu.SemaphoreType.DMA((32,))]
-        + exchange_scratch((width_pno, width_aux)),
-        compiler_params=params(49, 1),
-    )(
-        half,
-        jnp.pad(request[None, :], ((0, 7), (0, 128 - slots))),
-        pltpu.with_memory_space_constraint(pno_coef.reshape(halves, width_dom, width_pno), pltpu.HBM),
-        pltpu.with_memory_space_constraint(three_index, pltpu.HBM),
-    )
-    rows = rows.reshape(slots, width_pno, width_aux)
-
-    share = -(-pair_dev // planes)
-    gamma, energy_cols = pl.pallas_call(
-        couple_kernel,
-        name="couple_and_return_gamma",
-        out_shape=(
-            jax.ShapeDtypeStruct((CAPACITY, 4, 8, width_pno, width_aux), jnp.bfloat16),
-            jax.ShapeDtypeStruct((planes, share, width_pno), jnp.float32),
-        ),
-        in_specs=[smem] * 7 + [vmem] * 2,
-        out_specs=(hbm, vmem),
-        scratch_shapes=[
+        + [
             pltpu.VMEM((share, width_pno, width_pno), jnp.float32),
             pltpu.VMEM((planes - 1, share, width_pno, width_pno), jnp.bfloat16),
             pltpu.VMEM((planes - 1, share, width_pno, width_pno), jnp.bfloat16),
@@ -504,9 +508,16 @@
         ]
         + [pltpu.SemaphoreType.DMA((SUMMED_IN_PARTS * (planes - 1),))] * 4
         + [pltpu.SemaphoreType.DMA((planes - 1,))] * 2
-        + exchange_scratch((width_pno, width_aux)),
-        compiler_params=params(49, 2),
-    )(slot_of, half // 2, half % 2, partner, pair_occ.reshape(halves), pno_count, fock_diag, pno_energy, rows)
+        + row_block[:1]
+        + row_block[1:2] * 2
+        + row_block[2:] * 2,
+        compiler_params=params(56, 1),
+    )(
+        half, slot_of, half // 2, half % 2, partner, pair_occ.reshape(halves), pno_count, fock_diag,
+        jnp.pad(request[None, :], ((0, 7), (0, 128 - slots))), pno_energy,
+        pltpu.with_memory_space_constraint(pno_coef.reshape(halves, width_dom, width_pno), pltpu.HBM),
+        pltpu.with_memory_space_constraint(three_index, pltpu.HBM),
+    )
     energy = jnp.sum(energy_cols, axis=2).reshape(-1)[:pair_dev] / (width_pno * width_pno)
     grad = pl.pallas_call(
         grad_kernel,

time: 286 us -> 279 us (0.976)
  Pallas kernels: 276 us -> 270 us
    pallas_call x2 -> x1, Pallas kernels: 263 us -> 256 us  [local(): pl.pallas_call(pairs_kernel, name='pairs', out_shape=(jax.ShapeDtypeStruc...]
where the time goes in v5:
time: 279 us; the launch traced here: 276 us
  Pallas kernels  270 us (97%)
    pallas_call x1, Pallas kernels, local(): pl.pallas_call(pairs_kernel, name='pairs', out_shape=(jax.ShapeDtypeStruc...  256 us
    pallas_call x1, Pallas kernels, local(): pl.pallas_call(grad_kernel, name='add_terms', out_shape=jax.ShapeDtypeStr...  14 us

profile of v5, /device:TPU:0, one launch (start us, length us, event | category | flops | bytes accessed | tf_op | source)
XLA Modules:
  0.0 276.0 jit_solution(2218040648861971517)
XLA Ops:
  0.6 0.8 copy.18
  1.4 0.1 reshape.112.occ_ref
  1.5 0.0 copy-start.1
  1.5 0.2 convert_reduce_fusion
  1.7 0.0 copy-start.2
  1.7 0.1 reduce_sum.49
  1.9 0.1 rev.3
  1.9 0.1 mul.47
  2.0 0.6 select_reduce_fusion
  2.7 0.6 and_select_fusion.1
  3.3 0.6 pad.4.request_ref
  3.9 0.0 copy-done.1
  3.9 0.0 copy-done.2
  3.9 256.1 %pairs.1 = (bf16[2,4,8,128,512]{4,3,2,1,0:T(8,128)(2,1)}, bf16[4,2,4,8,64,128]{5,4,3,2,1,0:T(8,128)(2,1)}, s32[64]{0:T(128)}, f32[4,8,128]{2,1,0:T(8,128)}) custom-call(s32[64]{0:T(128)} %get-tuple-element.15.half_ref, s32[62]{0:T(128)} %copy-done.2, s32[64]{0:T(128)} %get-tuple-element.14.pair_ref, s32[64]{0:T(128)} %get-tuple-element.13.side_ref, ...), custom_call_target="tpu_custom_call" | custom-call | tf_op jit(solution)/shard_map/pairs/pallas_call | solution.py:476
  260.0 0.8 reduce_sum.52
  260.8 0.1 reshape.114
  260.9 0.5 slice_multiply_fusion
  261.4 0.0 copy-start
  261.4 0.6 copy-done
  262.0 14.0 %add_terms.1 = f32[16,256,512]{2,1,0:T(8,128)} custom-call(s32[64]{0:T(128)S(1)} %copy-done, bf16[4,2,4,8,64,128]{5,4,3,2,1,0:T(8,128)(2,1)} %get-tuple-element.8.coef_ref, bf16[2,4,8,128,512]{4,3,2,1,0:T(8,128)(2,1)} %get-tuple-element.9.gamma_ref), custom_call_target="tpu_custom_call" | custom-call | tf_op jit(solution)/shard_map/add_terms/pallas_call | solution.py:522
  (3 shorter events, 0.0 us)
Async XLA Ops:
  1.5 2.4 copy-start.1
  1.7 2.1 copy-start.2
  261.4 0.6 copy-start

commit v6 on v5

--- a/solution.py
+++ b/solution.py
@@ -11,7 +11,7 @@
 MESH = pl.DeviceIdType.MESH
 GROUP_ORDER = (1, 3, 2, 0)
 OWN_FIRST = (0, 1, 3, 2)
-SUMMED_IN_PARTS = 2
+SUMMED_IN_PARTS = 4
 
 
 def plan_slots(pair_occ, groups, occ_dev):

time: 279 us -> 278 us (level)
  no operation moved by 1% of the time
where the time goes in v6:
time: 278 us; the launch traced here: 276 us
  Pallas kernels  270 us (97%)
    pallas_call x1, Pallas kernels, local(): pl.pallas_call(pairs_kernel, name='pairs', out_shape=(jax.ShapeDtypeStruc...  256 us
    pallas_call x1, Pallas kernels, local(): pl.pallas_call(grad_kernel, name='add_terms', out_shape=jax.ShapeDtypeStr...  14 us

profile of v6, /device:TPU:0, one launch (start us, length us, event | category | flops | bytes accessed | tf_op | source)
XLA Modules:
  0.0 275.8 jit_solution(1340082166996503312)
XLA Ops:
  0.6 0.8 copy.18
  1.4 0.1 reshape.112.occ_ref
  1.5 0.0 copy-start.1
  1.5 0.2 convert_reduce_fusion
  1.7 0.0 copy-start.2
  1.7 0.1 reduce_sum.49
  1.9 0.1 rev.3
  1.9 0.1 mul.47
  2.0 0.6 select_reduce_fusion
  2.7 0.6 and_select_fusion.1
  3.3 0.6 pad.4.request_ref
  3.9 0.0 copy-done.1
  3.9 0.0 copy-done.2
  3.9 256.0 %pairs.1 = (bf16[2,4,8,128,512]{4,3,2,1,0:T(8,128)(2,1)}, bf16[4,2,4,8,64,128]{5,4,3,2,1,0:T(8,128)(2,1)}, s32[64]{0:T(128)}, f32[4,8,128]{2,1,0:T(8,128)}) custom-call(s32[64]{0:T(128)} %get-tuple-element.15.half_ref, s32[62]{0:T(128)} %copy-done.2, s32[64]{0:T(128)} %get-tuple-element.14.pair_ref, s32[64]{0:T(128)} %get-tuple-element.13.side_ref, ...), custom_call_target="tpu_custom_call" | custom-call | tf_op jit(solution)/shard_map/pairs/pallas_call | solution.py:476
  259.8 0.8 reduce_sum.52
  260.6 0.1 reshape.114
  260.7 0.5 slice_multiply_fusion
  261.2 0.0 copy-start
  261.2 0.6 copy-done
  261.8 14.0 %add_terms.1 = f32[16,256,512]{2,1,0:T(8,128)} custom-call(s32[64]{0:T(128)S(1)} %copy-done, bf16[4,2,4,8,64,128]{5,4,3,2,1,0:T(8,128)(2,1)} %get-tuple-element.8.coef_ref, bf16[2,4,8,128,512]{4,3,2,1,0:T(8,128)(2,1)} %get-tuple-element.9.gamma_ref), custom_call_target="tpu_custom_call" | custom-call | tf_op jit(solution)/shard_map/add_terms/pallas_call | solution.py:522
  (3 shorter events, 0.0 us)
Async XLA Ops:
  1.5 2.4 copy-start.1
  1.7 2.1 copy-start.2
  261.2 0.6 copy-start
